TPU v7x, 32 devices: a whole 2x2x4 slice. The times are simulated.
32 devices in a mesh: dp: 4 (over y, core), rep: 8 (over z, x).
Axes of the slice: x: 2, y: 2, z: 4, core: 2. Of those that a mesh axis runs over, the one named last changes fastest.
Arguments:
- images: bfloat16 [512, 50, 768], P(('dp', 'rep')), may hold values from -6 to 6
- qkv_weight: bfloat16 [768, 2304], replicated, may hold values from -0.21875 to 0.21875
- out_weight: bfloat16 [768, 768], replicated, may hold values from -0.625 to 0.625
- fc1_weight: bfloat16 [768, 3072], replicated, may hold values from -0.21875 to 0.21875
- fc1_bias: float32 [3072], replicated, may hold values from -3 to 3
- fc2_weight: bfloat16 [3072, 768], replicated, may hold values from -0.109375 to 0.109375
- ln1_gain: float32 [768], replicated, may hold values from 0.5 to 1.5
- ln1_bias: float32 [768], replicated, may hold values from -1 to 1
- ln2_gain: float32 [768], replicated, may hold values from 0.5 to 1.5
- ln2_bias: float32 [768], replicated, may hold values from -1 to 1
- post_gain: float32 [768], replicated, may hold values from 0.5 to 1.5
- post_bias: float32 [768], replicated, may hold values from -1 to 1
- image_proj: bfloat16 [768, 512], replicated, may hold values from -0.21875 to 0.21875
- text_feats: bfloat16 [1536, 512], P(('dp', 'rep')), may hold values from -6 to 6
- text_gain: float32 [512], replicated, may hold values from 0.5 to 1.5
- text_bias: float32 [512], replicated, may hold values from -1 to 1
- text_proj: bfloat16 [512, 512], replicated, may hold values from -0.25 to 0.25
- log_scale: float32 [1], replicated, may hold values from 3.4 to 4
- caption_counts: int32 [512], P(('dp', 'rep')), may hold values from 1 to 5, as said below
- positives: int32 [1536], P(('dp', 'rep')), may hold values from 0 to 511, as said below
Outputs:
- block_out: bfloat16 [512, 50, 768], P(('dp', 'rep'))
- loss: float32 [], replicated
- grad_images: float32 [512, 50, 768], P(('dp', 'rep'))
- grad_qkv_weight: float32 [768, 2304], P('rep', 'dp')
- grad_out_weight: float32 [768, 768], P('rep', 'dp')
- grad_fc1_weight: float32 [768, 3072], P('rep', 'dp')
- grad_fc1_bias: float32 [3072], replicated
- grad_fc2_weight: float32 [3072, 768], P('rep', 'dp')
- grad_ln1_gain: float32 [768], replicated
- grad_ln1_bias: float32 [768], replicated
- grad_ln2_gain: float32 [768], replicated
- grad_ln2_bias: float32 [768], replicated
- grad_post_gain: float32 [768], replicated
- grad_post_bias: float32 [768], replicated
- grad_image_proj: float32 [768, 512], P('rep', 'dp')
- grad_text_feats: float32 [1536, 512], P(('dp', 'rep'))
- grad_text_gain: float32 [512], replicated
- grad_text_bias: float32 [512], replicated
- grad_text_proj: float32 [512, 512], P('rep', 'dp')
- grad_log_scale: float32 [1], replicated
Inputs may be any that keep to these rules, and one draw needn't show every extreme that they name: caption_counts[i] is the number of captions c with positives[c] = i; the counts sum to 1536. `positives`: the captions of an image stand anywhere among all captions.
All inputs are finite; a program needn't handle non-finite values.
Results may differ from a plain program's by a relative error of at most 0.015.
The roundings to bfloat16 on the way count: a program that leaves them out, or rounds other values in their place, can miss the bound.
Values may be sent and summed in bfloat16 or wider, within the bound.
A program may use at most 192 MiB of HBM per device.

v0:
```python
import jax
import jax.numpy as jnp
from jax import lax
from jax.sharding import PartitionSpec as P

HEADS = 12
HDIM = 64


def matmul(left, right):
    return jnp.dot(left, right, preferred_element_type=jnp.float32)


def matmul_left(left, right):
    return lax.dot_general(
        left, right, (((0,), (0,)), ((), ())), preferred_element_type=jnp.float32
    )


def matmul_right(left, right):
    return lax.dot_general(
        left, right, (((1,), (1,)), ((), ())), preferred_element_type=jnp.float32
    )


def layer_norm(values, gain, bias):
    centered = values - jnp.mean(values, -1, keepdims=True)
    factor = lax.rsqrt(jnp.mean(centered * centered, -1, keepdims=True) + 1e-05)
    normed = centered * factor
    return (normed * gain + bias, normed, factor)


def norm_back(grad_out, normed, factor, gain):
    scaled = grad_out * gain
    grad_in = factor * (
        scaled
        - jnp.mean(scaled, -1, keepdims=True)
        - normed * jnp.mean(scaled * normed, -1, keepdims=True)
    )
    return (grad_in, jnp.sum(grad_out * normed, 0), jnp.sum(grad_out, 0))


def unit_rows(values):
    factor = lax.rsqrt(jnp.sum(values * values, -1, keepdims=True) + 1e-06)
    return (values * factor, factor)


def unit_back(grad_unit, unit, factor):
    return factor * (grad_unit - unit * jnp.sum(grad_unit * unit, -1, keepdims=True))


def row_logsumexp(values):
    top_value = jnp.max(values, 1, keepdims=True)
    return top_value[:, 0] + jnp.log(jnp.sum(jnp.exp(values - top_value), 1))


def shards(
    images,
    qkv_weight,
    out_weight,
    fc1_weight,
    fc1_bias,
    fc2_weight,
    ln1_gain,
    ln1_bias,
    ln2_gain,
    ln2_bias,
    post_gain,
    post_bias,
    image_proj,
    text_feats,
    text_gain,
    text_bias,
    text_proj,
    log_scale,
    caption_counts,
    positives,
):
    images_here, patches, model_width = images.shape
    row_count = images_here * patches
    resid = images.reshape(row_count, model_width).astype(jnp.float32)
    normed_one, unit_one, factor_one = layer_norm(resid, ln1_gain, ln1_bias)
    normed_in = normed_one.astype(jnp.bfloat16)
    packed = (
        matmul(normed_in, qkv_weight)
        .astype(jnp.bfloat16)
        .reshape(images_here, patches, 3, HEADS, HDIM)
    )
    query, keys, values = (packed[:, :, 0], packed[:, :, 1], packed[:, :, 2])
    scores = 0.125 * jnp.einsum("bqhd,bkhd->bhqk", query, keys, preferred_element_type=jnp.float32)
    score_peak = jnp.max(scores, -1, keepdims=True)
    score_lse = score_peak + jnp.log(jnp.sum(jnp.exp(scores - score_peak), -1, keepdims=True))
    attn_low = jnp.exp(scores - score_lse).astype(jnp.bfloat16)
    mixed = jnp.einsum("bhqk,bkhd->bqhd", attn_low, values, preferred_element_type=jnp.float32)
    mixed = mixed.reshape(row_count, model_width).astype(jnp.bfloat16)
    middle = resid + matmul(mixed, out_weight)
    normed_two, unit_two, factor_two = layer_norm(middle, ln2_gain, ln2_bias)
    normed_mid = normed_two.astype(jnp.bfloat16)
    hidden = matmul(normed_mid, fc1_weight) + fc1_bias
    gate_sig = jax.nn.sigmoid(1.702 * hidden)
    activation = (hidden * gate_sig).astype(jnp.bfloat16)
    block = middle + matmul(activation, fc2_weight)
    block_out = block.reshape(images_here, patches, model_width).astype(jnp.bfloat16)
    class_rows = block.reshape(images_here, patches, model_width)[:, 0, :]
    class_full, unit_post, factor_post = layer_norm(class_rows, post_gain, post_bias)
    class_norm = class_full.astype(jnp.bfloat16)
    image_unit, image_factor = unit_rows(matmul(class_norm, image_proj))
    image_low = image_unit.astype(jnp.bfloat16)
    text_full, unit_text, factor_text = layer_norm(
        text_feats.astype(jnp.float32), text_gain, text_bias
    )
    text_norm = text_full.astype(jnp.bfloat16)
    text_unit, text_factor = unit_rows(matmul(text_norm, text_proj))
    text_low = text_unit.astype(jnp.bfloat16)
    all_images, all_texts = (
        lax.all_gather(image_low, ("dp", "rep"), axis=0, tiled=True),
        lax.all_gather(text_low, ("dp", "rep"), axis=0, tiled=True),
    )
    all_positives = lax.all_gather(positives, ("dp", "rep"), axis=0, tiled=True)
    image_total = all_images.shape[0]
    caption_total = all_texts.shape[0]
    text_ratio = image_total / caption_total
    logit_scale = jnp.exp(log_scale[0])
    image_ids = lax.axis_index(("dp", "rep")) * images_here + jnp.arange(
        images_here, dtype=jnp.int32
    )
    counts = caption_counts.astype(jnp.float32)
    row_logits = logit_scale * matmul_right(image_low, all_texts)
    row_match = (all_positives[None, :] == image_ids[:, None]).astype(jnp.float32)
    row_lse = row_logsumexp(row_logits)
    image_loss = row_lse - jnp.sum(row_match * row_logits, 1) / counts
    col_logits = logit_scale * matmul_right(text_low, all_images)
    col_match = (positives[:, None] == jnp.arange(image_total, dtype=jnp.int32)[None, :]).astype(
        jnp.float32
    )
    col_lse = row_logsumexp(col_logits)
    caption_loss = col_lse - jnp.sum(col_match * col_logits, 1)
    grad_rows = (
        0.5 * (jnp.exp(row_logits - row_lse[:, None]) - row_match / counts[:, None])
    ).astype(jnp.bfloat16)
    grad_cols = (0.5 * text_ratio * (jnp.exp(col_logits - col_lse[:, None]) - col_match)).astype(
        jnp.bfloat16
    )
    total_part = 0.5 * jnp.sum(image_loss) + 0.5 * text_ratio * jnp.sum(caption_loss)
    scale_part = jnp.sum(grad_rows.astype(jnp.float32) * row_logits) + jnp.sum(
        grad_cols.astype(jnp.float32) * col_logits
    )
    total, scale_grad = lax.psum((total_part, scale_part), ("dp", "rep"))
    loss = total / image_total
    grad_log_scale = scale_grad.reshape(1)
    columns = grad_cols
    grad_image_unit = logit_scale * matmul(grad_rows, all_texts) + lax.psum_scatter(
        logit_scale * matmul_left(columns, text_low), ("dp", "rep"), scatter_dimension=0, tiled=True
    )
    columns = grad_rows
    grad_text_unit = logit_scale * matmul(grad_cols, all_images) + lax.psum_scatter(
        logit_scale * matmul_left(columns, image_low),
        ("dp", "rep"),
        scatter_dimension=0,
        tiled=True,
    )
    grad_image_embed = unit_back(grad_image_unit, image_unit, image_factor).astype(jnp.bfloat16)
    grad_image_proj = matmul_left(class_norm, grad_image_embed)
    grad_class, grad_post_gain, grad_post_bias = norm_back(
        matmul_right(grad_image_embed, image_proj), unit_post, factor_post, post_gain
    )
    grad_text_embed = unit_back(grad_text_unit, text_unit, text_factor).astype(jnp.bfloat16)
    grad_text_proj = matmul_left(text_norm, grad_text_embed)
    grad_text_feats, grad_text_gain, grad_text_bias = norm_back(
        matmul_right(grad_text_embed, text_proj), unit_text, factor_text, text_gain
    )
    grad_block = (
        jnp.zeros((images_here, patches, model_width), jnp.float32)
        .at[:, 0, :]
        .set(grad_class)
        .reshape(row_count, model_width)
    )
    grad_block_low = grad_block.astype(jnp.bfloat16)
    grad_activation = matmul_right(grad_block_low, fc2_weight)
    grad_hidden = (
        grad_activation * (gate_sig + 1.702 * hidden * gate_sig * (1.0 - gate_sig))
    ).astype(jnp.bfloat16)
    grad_fc1_bias = jnp.sum(grad_hidden.astype(jnp.float32), 0)
    grad_mid_norm, grad_ln2_gain, grad_ln2_bias = norm_back(
        matmul_right(grad_hidden, fc1_weight), unit_two, factor_two, ln2_gain
    )
    grad_middle = grad_block + grad_mid_norm
    grad_middle_low = grad_middle.astype(jnp.bfloat16)
    grad_out_weight = matmul_left(mixed, grad_middle_low)
    grad_mixed = (
        matmul_right(grad_middle_low, out_weight)
        .astype(jnp.bfloat16)
        .reshape(images_here, patches, HEADS, HDIM)
    )
    again_scores = 0.125 * jnp.einsum(
        "bqhd,bkhd->bhqk", query, keys, preferred_element_type=jnp.float32
    )
    attn_full = jnp.exp(again_scores - score_lse)
    grad_values = jnp.einsum(
        "bhqk,bqhd->bkhd", attn_low, grad_mixed, preferred_element_type=jnp.float32
    )
    grad_attn = jnp.einsum(
        "bqhd,bkhd->bhqk", grad_mixed, values, preferred_element_type=jnp.float32
    )
    grad_scores = (
        attn_full * (grad_attn - jnp.sum(grad_attn * attn_full, -1, keepdims=True))
    ).astype(jnp.bfloat16)
    grad_query = 0.125 * jnp.einsum(
        "bhqk,bkhd->bqhd", grad_scores, keys, preferred_element_type=jnp.float32
    )
    grad_keys = 0.125 * jnp.einsum(
        "bhqk,bqhd->bkhd", grad_scores, query, preferred_element_type=jnp.float32
    )
    grad_packed = (
        jnp.stack([grad_query, grad_keys, grad_values], 2)
        .reshape(row_count, 3 * model_width)
        .astype(jnp.bfloat16)
    )
    grad_qkv_weight = matmul_left(normed_in, grad_packed)
    grad_in_norm, grad_ln1_gain, grad_ln1_bias = norm_back(
        matmul_right(grad_packed, qkv_weight), unit_one, factor_one, ln1_gain
    )
    grad_images = (grad_middle + grad_in_norm).reshape(images_here, patches, model_width)
    grad_fc2_weight = matmul_left(activation, grad_block_low)
    grad_fc1_weight = matmul_left(normed_mid, grad_hidden)
    first_qkv, first_out, first_fc1, first_fc2, first_image, first_text = (
        lax.psum_scatter(grad_qkv_weight, "dp", scatter_dimension=1, tiled=True),
        lax.psum_scatter(grad_out_weight, "dp", scatter_dimension=1, tiled=True),
        lax.psum_scatter(grad_fc1_weight, "dp", scatter_dimension=1, tiled=True),
        lax.psum_scatter(grad_fc2_weight, "dp", scatter_dimension=1, tiled=True),
        lax.psum_scatter(grad_image_proj, "dp", scatter_dimension=1, tiled=True),
        lax.psum_scatter(grad_text_proj, "dp", scatter_dimension=1, tiled=True),
    )
    summed_qkv, summed_out, summed_fc1, summed_fc2, summed_image, summed_text = (
        lax.psum_scatter(first_qkv, "rep", scatter_dimension=0, tiled=True),
        lax.psum_scatter(first_out, "rep", scatter_dimension=0, tiled=True),
        lax.psum_scatter(first_fc1, "rep", scatter_dimension=0, tiled=True),
        lax.psum_scatter(first_fc2, "rep", scatter_dimension=0, tiled=True),
        lax.psum_scatter(first_image, "rep", scatter_dimension=0, tiled=True),
        lax.psum_scatter(first_text, "rep", scatter_dimension=0, tiled=True),
    )
    vector_sums = lax.psum(
        (
            grad_ln1_gain,
            grad_ln1_bias,
            grad_ln2_gain,
            grad_ln2_bias,
            grad_fc1_bias,
            grad_post_gain,
            grad_post_bias,
            grad_text_gain,
            grad_text_bias,
        ),
        ("dp", "rep"),
    )
    return (
        block_out,
        loss,
        grad_images,
        summed_qkv,
        summed_out,
        summed_fc1,
        vector_sums[4],
        summed_fc2,
        vector_sums[0],
        vector_sums[1],
        vector_sums[2],
        vector_sums[3],
        vector_sums[5],
        vector_sums[6],
        summed_image,
        grad_text_feats,
        vector_sums[7],
        vector_sums[8],
        summed_text,
        grad_log_scale,
    )


def solution(mesh):
    return jax.shard_map(
        shards,
        mesh=mesh,
        in_specs=(
            P(("dp", "rep"), None, None),
            P(),
            P(),
            P(),
            P(),
            P(),
            P(),
            P(),
            P(),
            P(),
            P(),
            P(),
            P(),
            P(("dp", "rep"), None),
            P(),
            P(),
            P(),
            P(),
            P(("dp", "rep")),
            P(("dp", "rep")),
        ),
        out_specs=(
            P(("dp", "rep"), None, None),
            P(),
            P(("dp", "rep"), None, None),
            P("rep", "dp"),
            P("rep", "dp"),
            P("rep", "dp"),
            P(),
            P("rep", "dp"),
            P(),
            P(),
            P(),
            P(),
            P(),
            P(),
            P("rep", "dp"),
            P(("dp", "rep"), None),
            P(),
            P(),
            P("rep", "dp"),
            P(),
        ),
        check_vma=False,
    )
```

profile of v0, /device:TPU:0, one launch (start us, length us, event | category | flops | bytes accessed | tf_op | source)
XLA Modules:
  0.0 1143.6 jit_solution(18061207876044312201)
XLA Ops:
  31.8 12.1 %reshape.281 = bf16[16,50,3,12,64]{4,3,2,1,0:T(8,128)(2,1)} reshape(bf16[800,2304]{1,0:T(8,128)(2,1)} %convolution_convert_fusion) | data formatting | bytes 7372800 | tf_op jit(solution)/shard_map/reshape | solution.py:87
  67.7 7.5 fusion.58
  89.5 72.6 %all_gather.11 = bf16[512,512]{1,0:T(8,128)(2,1)S(1)} all-gather(bf16[16,512]{1,0:T(8,128)(2,1)S(1)} %multiply_convert_fusion.7), channel_id=1, replica_groups=mesh['dp'=4,'rep'=8] {'dp','rep'}, dimensions={0}, use_global_device_ids=true | all-gather | bytes 540672 | tf_op jit(solution)/shard_map/all_gather | solution.py:116
  170.7 37.4 %all-reduce.1 = s32[1536]{0:T(1024)} all-reduce(s32[1536]{0:T(1024)} %dynamic-update-slice.3), channel_id=1, replica_groups=mesh['dp'=4,'rep'=8] {'dp','rep'}, use_global_device_ids=true, to_apply=%add.1 | all-reduce | flops 1536 | bytes 12288
  214.9 84.4 %reduce-scatter.19.cloned.1.call-done = f32[16,512]{1,0:T(8,128)} async-done(((f32[512,512]{1,0:T(8,128)}), f32[16,512]{1,0:T(8,128)}) %reduce-scatter.19.cloned.1.call-update) | async-done | bytes 32784 | tf_op jit(solution)/shard_map/reduce_scatter | solution.py:152
  311.8 11.8 %convert_reduce_fusion = (f32[3072]{0:T(1024)}, bf16[800,3072]{1,0:T(8,128)(2,1)S(1)}) fusion(f32[800,3072]{1,0:T(8,128)} %copy-done.63, f32[3072]{0:T(1024)} %param.26, bf16[3072,768]{1,0:T(8,128)(2,1)} %param.27, f32[800,768]{1,0:T(8,128)} %reshape.284), kind=kOutput, calls=%fused_computation.1 | convolution fusion | flops 3807433728 | bytes 21946368 | tf_op jit(solution)/shard_map/dot_general | solution.py:21
  323.7 9.4 multiply_reduce_fusion.2
  354.9 7.4 multiply_reduce_fusion
  378.4 25.1 %reduce-scatter.37.cloned.1.call-done = f32[48,512]{1,0:T(8,128)} async-done(((f32[1536,512]{1,0:T(8,128)}), f32[48,512]{1,0:T(8,128)}) %reduce-scatter.37.cloned.1.call-update) | async-done | bytes 98320 | tf_op jit(solution)/shard_map/reduce_scatter | solution.py:156
  425.9 9.1 copy.110
  435.0 13.0 %convert_element_type.145 = bf16[800,2304]{1,0:T(8,128)(2,1)} reshape(bf16[16,50,3,12,64]{4,3,2,1,0:T(8,128)(2,1)} %copy.110) | data formatting | bytes 7372800 | tf_op jit(solution)/shard_map/convert_element_type | solution.py:217
  448.0 9.2 fusion.63
  457.3 11.0 fusion.20
  468.4 10.8 fusion.57
  482.2 14.5 %reduce-scatter.39.cloned.1.call-done = f32[512,128]{1,0:T(8,128)} async-done(((f32[512,512]{1,0:T(8,128)}), f32[512,128]{1,0:T(8,128)}) %reduce-scatter.39.cloned.1.call-update) | async-done | bytes 262160 | tf_op jit(solution)/shard_map/reduce_scatter | solution.py:232
  496.8 66.2 %reduce-scatter.21.cloned.1.call-done = f32[768,576]{0,1:T(8,128)} async-done(((f32[768,2304]{0,1:T(8,128)}), f32[768,576]{0,1:T(8,128)}) %reduce-scatter.21.cloned.1.call-update) | async-done | bytes 1769488 | tf_op jit(solution)/shard_map/reduce_scatter | solution.py:227
  565.9 78.3 %reduce-scatter.29.cloned.1.call-done = f32[3072,192]{0,1:T(8,128)} async-done(((f32[3072,768]{0,1:T(8,128)}), f32[3072,192]{0,1:T(8,128)}) %reduce-scatter.29.cloned.1.call-update) | async-done | bytes 2359312 | tf_op jit(solution)/shard_map/reduce_scatter | solution.py:230
  644.3 81.2 %reduce-scatter.25.cloned.1.call-done = f32[768,768]{1,0:T(8,128)} async-done(((f32[768,3072]{1,0:T(8,128)}), f32[768,768]{1,0:T(8,128)}) %reduce-scatter.25.cloned.1.call-update) | async-done | bytes 2359312 | tf_op jit(solution)/shard_map/reduce_scatter | solution.py:229
  753.1 41.8 %all-reduce.2 = (f32[]{:T(128)}, f32[3072]{0:T(1024)}, f32[768]{0:T(1024)}, f32[768]{0:T(1024)}, f32[768]{0:T(1024)}, /*index=5*/f32[768]{0:T(1024)}, f32[768]{0...) all-reduce(f32[]{:T(128)S(6)} %add.247, ...), channel_id=1, replica_groups=mesh['dp'=4,'rep'=8] {'dp','rep'}, use_global_device_ids=true, to_apply=%region_20.0 | all-reduce | flops 8706 | bytes 69648 | tf_op jit(solution)/shard_map/psum | solution.py:148
  797.9 58.9 %reduce-scatter.45.cloned.1.call-done = f32[96,192]{1,0:T(8,128)} async-done(((f32[768,192]{1,0:T(8,128)}), f32[96,192]{1,0:T(8,128)}) %reduce-scatter.45.cloned.1.call-update) | async-done | bytes 73744
  856.8 64.0 %reduce-scatter.41.cloned.1.call-done = f32[64,128]{1,0:T(8,128)} async-done(((f32[512,128]{1,0:T(8,128)}), f32[64,128]{1,0:T(8,128)}) %reduce-scatter.41.cloned.1.call-update) | async-done | bytes 32784 | tf_op jit(solution)/shard_map/reduce_scatter | solution.py:240
  920.7 70.0 %reduce-scatter.43.cloned.1.call-done = f32[96,576]{1,0:T(8,128)} async-done(((f32[768,576]{1,0:T(8,128)}), f32[96,576]{1,0:T(8,128)}) %reduce-scatter.43.cloned.1.call-update) | async-done | bytes 221200
  990.7 72.4 %reduce-scatter.31.cloned.1.call-done = f32[384,192]{0,1:T(8,128)} async-done(((f32[3072,192]{0,1:T(8,128)}), f32[384,192]{0,1:T(8,128)}) %reduce-scatter.31.cloned.1.call-update) | async-done | bytes 294928 | tf_op jit(solution)/shard_map/reduce_scatter | solution.py:238
  1063.1 72.5 %reduce-scatter.27.cloned.1.call-done = f32[96,768]{1,0:T(8,128)} async-done(((f32[768,768]{1,0:T(8,128)}), f32[96,768]{1,0:T(8,128)}) %reduce-scatter.27.cloned.1.call-update) | async-done | bytes 294928 | tf_op jit(solution)/shard_map/reduce_scatter | solution.py:237
  (270 shorter events, 182.9 us)
Async XLA Ops:
  7.2 17.7 %copy-start = (bf16[768,2304]{1,0:T(8,128)(2,1)S(1)}, bf16[768,2304]{1,0:T(8,128)(2,1)}, u32[]{:S(2)}) copy-start(bf16[768,2304]{1,0:T(8,128)(2,1)} %param.23) | copy-start | bytes 10616836
  7.2 201.4 %all-gather.2.cloned.1.call-start = ((), (), s32[]{:S(2)}) async-start(), calls=%async_computation.14 | async-start | bytes 1622016 | tf_op jit(solution)/shard_map/all_gather | solution.py:117
  12.2 287.2 %reduce-scatter.19.cloned.1.call-start = ((), (), s32[]{:S(2)}) async-start(), calls=%async_computation.15 | async-start | bytes 1081344 | tf_op jit(solution)/shard_map/reduce_scatter | solution.py:152
  21.8 10.0 copy-start.36
  21.9 9.9 copy-start.41
  88.9 73.2 %copy-start.58 = (f32[16]{0:T(128)}, f32[16]{0:T(128)S(1)}, u32[]{:S(2)}) copy-start(f32[16]{0:T(128)S(1)} %add_rsqrt_fusion.4) | copy-start | bytes 196
  89.5 72.6 %copy-start.30 = (bf16[16,512]{1,0:T(8,128)(2,1)}, bf16[16,512]{1,0:T(8,128)(2,1)S(1)}, u32[]{:S(2)}) copy-start(bf16[16,512]{1,0:T(8,128)(2,1)S(1)} %multiply_convert_fusion.7) | copy-start | bytes 49156
  167.4 236.0 %reduce-scatter.37.cloned.1.call-start = ((), (), s32[]{:S(2)}) async-start(), calls=%async_computation.24 | async-start | bytes 3244032 | tf_op jit(solution)/shard_map/reduce_scatter | solution.py:156
  214.9 264.4 %reduce-scatter.33.cloned.1.call-start = ((), (), s32[]{:S(2)}) async-start(), calls=%async_computation.22 | async-start | bytes 1966080 | tf_op jit(solution)/shard_map/reduce_scatter | solution.py:231
  311.8 168.1 %reduce-scatter.23.cloned.1.call-start = ((), (), s32[]{:S(2)}) async-start(), calls=%async_computation.17 | async-start | bytes 2949120 | tf_op jit(solution)/shard_map/reduce_scatter | solution.py:228
  311.8 11.8 %copy-start.9 = (f32[800,768]{1,0:T(8,128)S(1)}, f32[800,768]{1,0:T(8,128)}, u32[]{:S(2)}) copy-start(f32[800,768]{1,0:T(8,128)} %copy-done.8) | copy-start | bytes 7372804
  323.7 9.4 copy-start.13
  338.5 158.3 %reduce-scatter.39.cloned.1.call-start = ((), (), s32[]{:S(2)}) async-start(), calls=%async_computation.25 | async-start | bytes 1310720 | tf_op jit(solution)/shard_map/reduce_scatter | solution.py:232
  408.8 154.2 %reduce-scatter.21.cloned.1.call-start = ((), (), s32[]{:S(2)}) async-start(), calls=%async_computation.16 | async-start | bytes 8847360 | tf_op jit(solution)/shard_map/reduce_scatter | solution.py:227
  457.3 187.0 %reduce-scatter.29.cloned.1.call-start = ((), (), s32[]{:S(2)}) async-start(), calls=%async_computation.20 | async-start | bytes 11796480 | tf_op jit(solution)/shard_map/reduce_scatter | solution.py:230
  468.4 257.1 %reduce-scatter.25.cloned.1.call-start = ((), (), s32[]{:S(2)}) async-start(), calls=%async_computation.18 | async-start | bytes 11796480 | tf_op jit(solution)/shard_map/reduce_scatter | solution.py:229
  479.2 318.7 %reduce-scatter.35.cloned.1.call-start = ((), (), s32[]{:S(2)}) async-start(), calls=%async_computation.23 | async-start | bytes 442368 | tf_op jit(solution)/shard_map/reduce_scatter | solution.py:239
  479.8 377.0 %reduce-scatter.45.cloned.1.call-start = ((), (), s32[]{:S(2)}) async-start(), calls=%async_computation.28 | async-start | bytes 884736
  482.2 438.6 %reduce-scatter.41.cloned.1.call-start = ((), (), s32[]{:S(2)}) async-start(), calls=%async_computation.26 | async-start | bytes 294912 | tf_op jit(solution)/shard_map/reduce_scatter | solution.py:240
  496.7 494.0 %reduce-scatter.43.cloned.1.call-start = ((), (), s32[]{:S(2)}) async-start(), calls=%async_computation.27 | async-start | bytes 2211840
  565.9 497.2 %reduce-scatter.31.cloned.1.call-start = ((), (), s32[]{:S(2)}) async-start(), calls=%async_computation.21 | async-start | bytes 2654208 | tf_op jit(solution)/shard_map/reduce_scatter | solution.py:238
  644.3 491.3 %reduce-scatter.27.cloned.1.call-start = ((), (), s32[]{:S(2)}) async-start(), calls=%async_computation.19 | async-start | bytes 2654208 | tf_op jit(solution)/shard_map/reduce_scatter | solution.py:237
  743.0 10.1 copy-start.43
  743.0 10.1 copy-start.44
  (59 other events, 235.9 us)
Sparse Core Ops, SparseCore 0:
  12.3 57.7 all-gather.1
  167.6 131.7 reduce-scatter.18
  305.7 97.7 reduce-scatter.36
  406.0 27.1 reduce-scatter.32
  435.6 33.0 reduce-scatter.22
  471.8 24.8 reduce-scatter.38
  499.2 63.7 reduce-scatter.20
  565.8 78.4 reduce-scatter.28
  647.0 78.4 reduce-scatter.24
  729.5 61.4 reduce-scatter.34
  795.2 61.5 reduce-scatter.44
  860.5 60.1 reduce-scatter.40
  924.8 65.8 reduce-scatter.42
  995.0 67.9 reduce-scatter.30
  1067.4 68.1 reduce-scatter.26
where the time goes:
time: 1160 us; the launch traced here: 1140 us
  waiting for transfers between devices  688 us (59%)
  blocking collectives  152 us (13%)
  matrix products  138 us (12%)
  local copies, waits for them, and re-layouts  98.4 us (8%)
  other arithmetic  46.2 us (4%)
  between operations  20.3 us (2%)
    unnamed x17, waiting for transfers between devices  130 us
    reduce_scatter x1, waiting for transfers between devices, shards(): lax.psum_scatter(logit_scale * matmul_left(columns, text_low), ('dp', 're...  84.4 us
    reduce_scatter x1, waiting for transfers between devices, shards(): lax.psum_scatter(grad_fc1_weight, 'dp', scatter_dimension=1, tiled=True)  81.2 us
    reduce_scatter x1, waiting for transfers between devices, shards(): lax.psum_scatter(grad_fc2_weight, 'dp', scatter_dimension=1, tiled=True)  78.3 us
    all_gather x1, blocking collectives, shards(): lax.all_gather(image_low, ('dp', 'rep'), axis=0, tiled=True)  72.6 us
    reduce_scatter x1, waiting for transfers between devices, shards(): lax.psum_scatter(first_fc1, 'rep', scatter_dimension=0, tiled=True)  72.5 us
    reduce_scatter x1, waiting for transfers between devices, shards(): lax.psum_scatter(first_fc2, 'rep', scatter_dimension=0, tiled=True)  72.4 us
    reduce_scatter x1, waiting for transfers between devices, shards(): lax.psum_scatter(grad_qkv_weight, 'dp', scatter_dimension=1, tiled=True)  66.2 us
  transfers between devices with their start and end apart: 15, of which 11 were waited for; matrix products, arithmetic and copies ran while one was open for 24% of the time, Pallas kernels for 0%

commit v1 on v0

--- a/solution.py
+++ b/solution.py
@@ -1,6 +1,10 @@
+import functools
+
 import jax
 import jax.numpy as jnp
 from jax import lax
+from jax.experimental import pallas as pl
+from jax.experimental.pallas import tpu as pltpu
 from jax.sharding import PartitionSpec as P
 
 HEADS = 12
@@ -277,9 +281,706 @@
     )
 
 
+MESH = pl.DeviceIdType.MESH
+F32 = jnp.float32
+BF16 = jnp.bfloat16
+PATCHES = 50
+WIDTH = 768
+HIDDEN = 3072
+EMBED = 512
+GROUP = 8
+STEP = 160
+
+
+def fits(dp_size, rep_size):
+    return dp_size == 4 and rep_size == 8
+
+
+def dot_rows(left, right):
+    return lax.dot_general(left, right, (((1,), (1,)), ((), ())), preferred_element_type=F32)
+
+
+def dot_cols(left, right):
+    return lax.dot_general(left, right, (((0,), (0,)), ((), ())), preferred_element_type=F32)
+
+
+def lane_shift(values, amount):
+    width = values.shape[1]
+    amount = amount % width
+    return values if amount == 0 else pltpu.roll(values, width - amount, 1)
+
+
+def pick_blocks(values, side, sides, block, count):
+    lanes = block * count
+    place = lax.broadcasted_iota(jnp.int32, (values.shape[0], lanes), 1) // block
+    picked = lane_shift(values, side * block)[:, :lanes]
+    for index in range(1, count):
+        offset = (side + index * sides) * block - index * block
+        picked = jnp.where(place == index, lane_shift(values, offset)[:, :lanes], picked)
+    return picked
+
+
+def head_spread(rows):
+    count = rows.shape[0]
+    lane_head = lax.broadcasted_iota(jnp.int32, (HEADS, count, WIDTH), 2) // HDIM
+    head = lax.broadcasted_iota(jnp.int32, (HEADS, count, WIDTH), 0)
+    spread = jnp.where(lane_head == head, rows[None], 0.0)
+    return spread.reshape(HEADS * count, WIDTH)
+
+
+def head_gather(stacked):
+    count = stacked.shape[0] // HEADS
+    stacked = stacked.reshape(HEADS, count, WIDTH)
+    lane_head = lax.broadcasted_iota(jnp.int32, stacked.shape, 2) // HDIM
+    head = lax.broadcasted_iota(jnp.int32, stacked.shape, 0)
+    return jnp.sum(jnp.where(lane_head == head, stacked, 0.0), 0)
+
+
+def fused_kernel(dims, counter, *refs):
+    (
+        x, qkv_hbm, out_hbm, fc1_hbm, fc2_hbm, ip_hbm, tp_hbm, fc1_bias,
+        ln1_gain, ln1_bias, ln2_gain, ln2_bias, post_gain, post_bias,
+        text_feats, text_gain, text_bias, log_scale, caption_counts, positives,
+        block_out, grad_images, g_qkv, g_out, g_fc1, g_fc2, g_ip, g_text, g_tp, g_vec,
+        qkv, w_out, fc1, fc2, ip, tp,
+        ni, kv, qd, mixed, middle, nmd, ff_acc, gni,
+        attn, attn_low, gsp, uu,
+        hid_c, small,
+        t_all, pos_all, i_all, cnt_all, row_sum, col_sum,
+        gi_send, gi_recv, gt_send, gt_recv,
+        nm_full, gb_full, rf_out, rf_in, ro_out, ro_in, tn_out, tn_in,
+        co_out, co_in, te_out, te_in, ps_send, ps_recv, pt_send, pt_recv,
+        vec_z, vec_p, hid_s, act_s, gh_s, nm_sel,
+        local_sem, send_sem, recv_sem,
+    ) = refs
+    images_here, captions_here, planes, sides, dp_size = dims
+    plane_size = dp_size * sides
+    rep_size = planes * sides
+    rows_all = images_here * PATCHES
+    half = rows_all // 2
+    dp = lax.axis_index("dp")
+    rep = lax.axis_index("rep")
+    z = rep // sides
+    side = lax.rem(rep, sides)
+    slot = dp * sides + side
+    plane_images = plane_size * images_here
+    line_captions = planes * captions_here
+    image_total = plane_images * planes
+    caption_total = line_captions * plane_size
+    text_ratio = image_total / caption_total
+
+    used = [0]
+
+    def plane_peer(step):
+        peer = lax.rem(slot + step, plane_size)
+        return peer, (peer // sides, z * sides + lax.rem(peer, sides))
+
+    def line_peer(step):
+        peer = lax.rem(z + step, planes)
+        return peer, (dp, peer * sides + side)
+
+    def copy_to(source, target, device):
+        index = used[0]
+        used[0] += 1
+        return pltpu.make_async_remote_copy(
+            src_ref=source, dst_ref=target, send_sem=send_sem.at[index], recv_sem=recv_sem.at[index],
+            device_id=device, device_id_type=MESH,
+        )
+
+    def to_plane(source_of, target):
+        copies = []
+        for step in range(1, plane_size):
+            peer, device = plane_peer(step)
+            copies.append(copy_to(source_of(peer), target, device))
+        for copy in copies:
+            copy.start()
+        return copies
+
+    def to_line(source_of, target):
+        copies = []
+        for step in range(1, planes):
+            peer, device = line_peer(step)
+            copies.append(copy_to(source_of(peer), target, device))
+        for copy in copies:
+            copy.start()
+        return copies
+
+    def finish(copies):
+        for copy in copies:
+            copy.wait()
+
+    loads = []
+    for index, (source, target) in enumerate(
+        ((tp_hbm, tp), (qkv_hbm, qkv), (out_hbm, w_out), (fc1_hbm, fc1), (fc2_hbm, fc2), (ip_hbm, ip))
+    ):
+        load = pltpu.make_async_copy(source, target, local_sem.at[index])
+        load.start()
+        loads.append(load)
+
+    barrier = pltpu.get_barrier_semaphore()
+    for step in range(1, plane_size):
+        pl.semaphore_signal(barrier, inc=1, device_id=plane_peer(step)[1], device_id_type=MESH)
+    for step in range(1, planes):
+        pl.semaphore_signal(barrier, inc=1, device_id=line_peer(step)[1], device_id_type=MESH)
+
+    text_full, _, _ = layer_norm(text_feats[...].astype(F32), text_gain[...], text_bias[...])
+    text_norm = text_full.astype(BF16)
+    loads[0].wait()
+    text_unit, text_factor = unit_rows(matmul(text_norm, tp[...]))
+    t_all[z] = text_unit.astype(BF16)
+    pos_rows = jnp.broadcast_to(positives[...].astype(F32), (128, captions_here))
+    pos_all[z] = jnp.transpose(pos_rows)
+    cnt_rows = jnp.broadcast_to(caption_counts[...].astype(F32), (128, images_here))
+    cnt_all[slot] = jnp.transpose(cnt_rows)
+    pl.semaphore_wait(barrier, plane_size - 1 + planes - 1)
+    text_copies = to_line(lambda peer: t_all.at[z], t_all.at[z])
+    pos_copies = to_line(lambda peer: pos_all.at[z], pos_all.at[z])
+    cnt_copies = to_plane(lambda peer: cnt_all.at[slot], cnt_all.at[slot])
+
+    def norm_in(step, _):
+        rows = pl.ds(pl.multiple_of(step * STEP, STEP), STEP)
+        full, _, _ = layer_norm(x[rows, :].astype(F32), ln1_gain[...], ln1_bias[...])
+        full = full.reshape(STEP // 16, 2, GROUP, WIDTH)
+        for part in range(2):
+            to = pl.ds(pl.multiple_of(part * half + step * (STEP // 2), 16), STEP // 2)
+            ni[to, :] = full[:, part].reshape(STEP // 2, WIDTH).astype(BF16)
+        return 0
+
+    lax.fori_loop(0, rows_all // STEP, norm_in, 0)
+
+    loads[1].wait()
+
+    def keys_values(step, _):
+        source = pl.ds(pl.multiple_of(WIDTH + step * 256, 256), 256)
+        to = pl.ds(pl.multiple_of(step * 256, 256), 256)
+        kv[:, to] = matmul(ni[...], qkv[:, source]).astype(BF16)
+        return 0
+
+    lax.fori_loop(0, 2 * WIDTH // 256, keys_values, 0)
+
+    resid_c = x[0:images_here, :].astype(F32)
+    normed_c = layer_norm(resid_c, ln1_gain[...], ln1_bias[...])[0].astype(BF16)
+    query_c = matmul(normed_c, qkv[:, 0:WIDTH]).astype(BF16)
+    query_spread = head_spread(query_c.astype(F32)).astype(BF16)
+    scores = 0.125 * dot_rows(query_spread, kv[:, 0:WIDTH])
+    row_image = lax.rem(lax.broadcasted_iota(jnp.int32, scores.shape, 0), images_here)
+    column = lax.broadcasted_iota(jnp.int32, scores.shape, 1)
+    column_image = jnp.where(column < half, 0, GROUP) + lax.rem(column, GROUP)
+    scores = jnp.where(row_image == column_image, scores, -1e30)
+    weights = jnp.exp(scores - jnp.max(scores, 1, keepdims=True))
+    weights = weights * (1.0 / jnp.sum(weights, 1, keepdims=True))
+    attn[...] = weights
+    attn_low[...] = weights.astype(BF16)
+    mixed_c = head_gather(matmul(attn_low[...], kv[:, WIDTH:]))
+    loads[2].wait()
+    middle_c = resid_c + matmul(mixed_c.astype(BF16), w_out[...])
+    full, unit_two, factor_two = layer_norm(middle_c, ln2_gain[...], ln2_bias[...])
+    nm_full[z, slot] = full.astype(BF16)
+    nm_line = to_line(lambda peer: nm_full.at[z, slot], nm_full.at[z, slot])
+    loads[3].wait()
+    hid_c[...] = matmul(full.astype(BF16), fc1[...]) + fc1_bias[...]
+    act_c = (hid_c[...] * jax.nn.sigmoid(1.702 * hid_c[...])).astype(BF16)
+    loads[4].wait()
+    block_c = middle_c + matmul(act_c, fc2[...])
+    full, unit_post, factor_post = layer_norm(block_c, post_gain[...], post_bias[...])
+    class_norm = full.astype(BF16)
+    loads[5].wait()
+    image_unit, image_factor = unit_rows(matmul(class_norm, ip[...]))
+    i_all[slot] = image_unit.astype(BF16)
+    image_copies = to_plane(lambda peer: i_all.at[slot], i_all.at[slot])
+    small[0] = unit_two
+    small[1] = unit_post
+
+    value_rows = matmul(attn_low[...], ni[...])
+    normed_cf = normed_c.astype(F32)
+    block_lanes = WIDTH // rep_size
+    text_lanes = EMBED // rep_size
+    for to_side in range(sides):
+        picked = pick_blocks(value_rows, to_side, sides, block_lanes, planes).astype(BF16)
+        rf_out[to_side, 2 * HEADS : 3 * HEADS] = picked.reshape(HEADS, images_here, planes * block_lanes)
+        picked = pick_blocks(normed_cf, to_side, sides, block_lanes, planes).astype(BF16)
+        rf_out[to_side, 0:HEADS] = jnp.broadcast_to(picked[None], (HEADS, images_here, planes * block_lanes))
+        ro_out[to_side, 0] = pick_blocks(mixed_c, to_side, sides, block_lanes, planes).astype(BF16)
+        ro_out[to_side, 1] = pick_blocks(full, to_side, sides, block_lanes, planes).astype(BF16)
+        tn_out[to_side] = pick_blocks(text_full, to_side, sides, text_lanes, planes).astype(BF16)
+
+    heads_here = 3 * HEADS // dp_size
+    bundle = heads_here // 3
+    rf_copies = []
+    for step in range(1, plane_size):
+        peer, device = plane_peer(step)
+        for part in range(3):
+            first = (peer // sides) * heads_here + part * bundle
+            mine = dp * heads_here + part * bundle
+            copy = copy_to(
+                rf_out.at[lax.rem(peer, sides), pl.ds(first, bundle)],
+                rf_in.at[pl.ds(part * bundle, bundle), slot], device,
+            )
+            is_keys = (first >= HEADS) & (first < 2 * HEADS)
+            mine_keys = (mine >= HEADS) & (mine < 2 * HEADS)
+            rf_copies.append((copy, is_keys, mine_keys))
+
+    for copy, is_keys, _ in rf_copies:
+        pl.when(jnp.logical_not(is_keys))(copy.start)
+    ro_copies = to_plane(lambda peer: ro_out.at[lax.rem(peer, sides)], ro_in.at[:, slot])
+    tn_copies = to_plane(lambda peer: tn_out.at[lax.rem(peer, sides)], tn_in.at[slot])
+
+    def dense_query():
+        def piece(step, _):
+            columns = pl.ds(pl.multiple_of(step * 256, 256), 256)
+            qd[:, columns] = (0.125 * matmul(ni[...], qkv[:, columns]).astype(BF16).astype(F32)).astype(BF16)
+            return 0
+
+        lax.fori_loop(0, WIDTH // 256, piece, 0)
+
+    def dense_attention(first, last):
+        def piece(index, _):
+            part = index // (HEADS // 2)
+            pair = lax.rem(index, HEADS // 2)
+            rows = pl.ds(pl.multiple_of(part * half, 16), half)
+            lanes = pl.ds(pl.multiple_of(pair * 128, 128), 128)
+            value_lanes = pl.ds(pl.multiple_of(WIDTH + pair * 128, 128), 128)
+            query = qd[rows, lanes]
+            keys = kv[rows, lanes]
+            values = kv[rows, value_lanes]
+            lane = lax.broadcasted_iota(jnp.int32, (half, 128), 1)
+            row_of = lax.rem(lax.broadcasted_iota(jnp.int32, (half, half), 0), GROUP)
+            col_of = lax.rem(lax.broadcasted_iota(jnp.int32, (half, half), 1), GROUP)
+            same = row_of == col_of
+            result = None
+            for which in range(2):
+                own = (lane < HDIM) if which == 0 else (lane >= HDIM)
+                logits = dot_rows(jnp.where(own, query, jnp.zeros_like(query)), keys)
+                logits = jnp.where(same, logits, -1e30)
+                top = jnp.exp(logits - jnp.max(logits, 1, keepdims=True))
+                top = top * (1.0 / jnp.sum(top, 1, keepdims=True))
+                got = matmul(top.astype(BF16), values)
+                result = got if which == 0 else jnp.where(own, got, result)
+            mixed[rows, lanes] = result.astype(BF16)
+            return 0
+
+        lax.fori_loop(first, last, piece, 0)
+
+    def dense_out():
+        def piece(step, _):
+            parts = []
+            for part in range(2):
+                rows = pl.ds(pl.multiple_of(part * half + step * (STEP // 2), 16), STEP // 2)
+                parts.append(matmul(mixed[rows, :], w_out[...]).reshape(STEP // 16, GROUP, WIDTH))
+            joined = jnp.stack(parts, 1).reshape(STEP, WIDTH)
+            rows = pl.ds(pl.multiple_of(step * STEP, STEP), STEP)
+            value = x[rows, :].astype(F32) + joined
+            middle[rows, :] = value
+            nmd[rows, :] = layer_norm(value, ln2_gain[...], ln2_bias[...])[0].astype(BF16)
+            return 0
+
+        lax.fori_loop(0, rows_all // STEP, piece, 0)
+
+    def dense_ff():
+        def outer(part, _):
+            rows = pl.ds(pl.multiple_of(part * half, 16), half)
+            ff_acc[...] = middle[rows, :]
+
+            def inner(step, _):
+                columns = pl.ds(pl.multiple_of(step * 768, 768), 768)
+                hidden = matmul(nmd[rows, :], fc1[:, columns]) + fc1_bias[:, columns]
+                act = (hidden * jax.nn.sigmoid(1.702 * hidden)).astype(BF16)
+                ff_acc[...] += matmul(act, fc2[columns, :])
+                return 0
+
+            lax.fori_loop(0, HIDDEN // 768, inner, 0)
+            block_out[rows, :] = ff_acc[...].astype(BF16)
+            return 0
+
+        lax.fori_loop(0, 2, outer, 0)
+
+    dense_query()
+
+    finish(text_copies)
+    finish(pos_copies)
+    finish(cnt_copies)
+    finish(image_copies)
+    scale = jnp.exp(log_scale[...])
+    images_low = i_all[...].reshape(plane_images, EMBED)
+    texts_low = t_all[...].reshape(line_captions, EMBED)
+    logits = scale * dot_rows(images_low, texts_low)
+    logits_t = scale * dot_rows(texts_low, images_low)
+
+    def image_ids(dim, shape):
+        index = lax.broadcasted_iota(jnp.int32, shape, dim)
+        holder = index // images_here
+        owner = (holder // sides) * rep_size + z * sides + lax.rem(holder, sides)
+        return (owner * images_here + lax.rem(index, images_here)).astype(F32)
+
+    pos_col = pos_all[...].reshape(line_captions, 128)
+    match_t = (pos_col[:, 0:1] == image_ids(1, logits_t.shape)).astype(F32)
+    match = (jnp.transpose(pos_col) == image_ids(0, logits.shape)).astype(F32)
+    counts = jnp.transpose(cnt_all[...].reshape(plane_images, 128))[0:1, :]
+    row_sum[slot] = jnp.broadcast_to(jnp.sum(jnp.exp(logits_t), 0, keepdims=True), (8, plane_images))
+    col_sum[z] = jnp.broadcast_to(jnp.sum(jnp.exp(logits), 0, keepdims=True), (8, line_captions))
+    sum_copies = to_plane(lambda peer: row_sum.at[slot], row_sum.at[slot])
+    sum_copies += to_line(lambda peer: col_sum.at[z], col_sum.at[z])
+
+    finish(nm_line)
+    nm_plane = to_plane(lambda peer: nm_full.at[:, slot], nm_full.at[:, slot])
+    dense_attention(0, 3)
+
+    finish(sum_copies)
+    row_lse = jnp.log(jnp.sum(row_sum[...], 0)[0:1])
+    col_lse = jnp.log(jnp.sum(col_sum[...], 0)[0:1])
+    grad_cols = (0.5 * text_ratio * (jnp.exp(logits - col_lse) - match)).astype(BF16)
+    grad_rows_t = (0.5 * (jnp.exp(logits_t - row_lse) - match_t / counts)).astype(BF16)
+    loss_part = 0.5 * (jnp.sum(row_lse) / plane_size - jnp.sum(match_t * logits_t / counts)) + (
+        0.5 * text_ratio
+    ) * (jnp.sum(col_lse) / planes - jnp.sum(match * logits))
+    scale_part = jnp.sum(grad_cols.astype(F32) * logits) + jnp.sum(grad_rows_t.astype(F32) * logits_t)
+    gi_send[...] = (scale * (dot_cols(grad_rows_t, texts_low) + matmul(grad_cols, texts_low))).reshape(
+        plane_size, images_here, EMBED
+    )
+    gi_copies = to_plane(lambda peer: gi_send.at[peer], gi_recv.at[slot])
+    gi_recv[slot] = gi_send[slot]
+    gt_send[...] = (scale * (dot_cols(grad_cols, images_low) + matmul(grad_rows_t, images_low))).reshape(
+        planes, captions_here, EMBED
+    )
+    gt_copies = to_line(lambda peer: gt_send.at[peer], gt_recv.at[z])
+    gt_recv[z] = gt_send[z]
+
+    dense_attention(3, 6)
+
+    finish(gi_copies)
+    grad_embed = unit_back(jnp.sum(gi_recv[...], 0), image_unit, image_factor).astype(BF16)
+    grad_class, g_post_gain, g_post_bias = norm_back(
+        dot_rows(grad_embed, ip[...]), small[1], factor_post, post_gain[...]
+    )
+    gb_low = grad_class.astype(BF16)
+    gb_full[z, slot] = gb_low
+    gb_line = to_line(lambda peer: gb_full.at[z, slot], gb_full.at[z, slot])
+    gate = jax.nn.sigmoid(1.702 * hid_c[...])
+    grad_hidden = (
+        dot_rows(gb_low, fc2[...]) * (gate + 1.702 * hid_c[...] * gate * (1.0 - gate))
+    ).astype(BF16)
+    g_fc1_bias = jnp.sum(grad_hidden.astype(F32), 0, keepdims=True)
+    grad_two, g_ln2_gain, g_ln2_bias = norm_back(
+        dot_rows(grad_hidden, fc1[...]), small[0], factor_two, ln2_gain[...]
+    )
+    grad_middle = grad_class + grad_two
+    grad_middle_low = grad_middle.astype(BF16)
+    grad_mixed = dot_rows(grad_middle_low, w_out[...]).astype(BF16)
+    mixed_spread = head_spread(grad_mixed.astype(F32)).astype(BF16)
+    grad_attn = dot_rows(mixed_spread, kv[:, WIDTH:])
+    weights = attn[...]
+    grad_scores = weights * (grad_attn - jnp.sum(grad_attn * weights, 1, keepdims=True))
+    grad_scores = 0.125 * grad_scores.astype(BF16).astype(F32)
+    gsp[0 : HEADS * images_here] = grad_scores.astype(BF16)
+    gsp[HEADS * images_here :] = attn_low[...]
+    score_low = gsp[0 : HEADS * images_here]
+    grad_query = head_gather(matmul(score_low, kv[:, 0:WIDTH])).astype(BF16)
+    key_rows = matmul(score_low, ni[...])
+    for to_side in range(sides):
+        picked = pick_blocks(key_rows, to_side, sides, block_lanes, planes).astype(BF16)
+        rf_out[to_side, HEADS : 2 * HEADS] = picked.reshape(HEADS, images_here, planes * block_lanes)
+
+    grad_q = grad_query.astype(F32)
+    query_f = query_c.astype(F32)
+    grad_v = grad_mixed.astype(F32)
+    lane = lax.broadcasted_iota(jnp.int32, (images_here, 128), 1)
+    q_shift, k_shift, v_shift = lane_shift(grad_q, 64), lane_shift(query_f, -64), lane_shift(grad_v, 64)
+    m_shift = lane_shift(grad_middle_low.astype(F32), 64)
+    m_plain = grad_middle_low.astype(F32)
+    co_out[0, :, 0:576] = grad_q[:, 0:576].astype(BF16)
+    co_out[1, :, 0:128] = q_shift[:, 512:640].astype(BF16)
+    co_out[1, :, 128:256] = jnp.where(lane < 64, q_shift[:, 640:768], k_shift[:, 0:128]).astype(BF16)
+    co_out[1, :, 256:576] = k_shift[:, 128:448].astype(BF16)
+    co_out[2, :, 0:384] = query_f[:, 384:768].astype(BF16)
+    co_out[2, :, 384:576] = grad_v[:, 0:192].astype(BF16)
+    co_out[3, :, 0:576] = v_shift[:, 128:704].astype(BF16)
+    for to_dp, source in enumerate((m_plain[:, 0:192], m_shift[:, 128:320], m_plain[:, 384:576], m_shift[:, 512:704])):
+        co_out[to_dp, :, 640:832] = source.astype(BF16)
+        co_out[to_dp, :, 896:1024] = grad_embed[:, to_dp * 128 : to_dp * 128 + 128]
+    co_copies = to_plane(lambda peer: co_out.at[peer // sides], co_in.at[slot])
+    for copy, is_keys, _ in rf_copies:
+        pl.when(is_keys)(copy.start)
+    own_rf = pltpu.make_async_copy(
+        rf_out.at[side, pl.ds(dp * heads_here, heads_here)], rf_in.at[:, slot], local_sem.at[6]
+    )
+    own_rf.start()
+    co_in[slot] = co_out[dp]
+    ro_in[:, slot] = ro_out[side]
+    tn_in[slot] = tn_out[side]
+
+    finish(gt_copies)
+    grad_text = unit_back(jnp.sum(gt_recv[...], 0), text_unit, text_factor).astype(BF16)
+    for to_dp in range(dp_size):
+        te_out[to_dp] = grad_text[:, to_dp * 128 : to_dp * 128 + 128]
+    te_copies = to_plane(lambda peer: te_out.at[peer // sides], te_in.at[slot])
+    te_in[slot] = te_out[dp]
+    _, unit_text, factor_text = layer_norm(text_feats[...].astype(F32), text_gain[...], text_bias[...])
+    g_feats, g_text_gain, g_text_bias = norm_back(
+        dot_rows(grad_text, tp[...]), unit_text, factor_text, text_gain[...]
+    )
+    g_text[...] = g_feats
+
+    finish(gb_line)
+    gb_plane = to_plane(lambda peer: gb_full.at[:, slot], gb_full.at[:, slot])
+
+    uu[0 : HEADS * images_here] = dot_rows(query_spread, qkv[:, WIDTH : 2 * WIDTH]).astype(BF16)
+    uu[HEADS * images_here :] = dot_rows(mixed_spread, qkv[:, 2 * WIDTH :]).astype(BF16)
+    class_in = dot_rows(grad_query, qkv[:, 0:WIDTH])
+
+    def spread_back(step, _):
+        columns = pl.ds(pl.multiple_of(step * 256, 256), 256)
+        gni[:, columns] = dot_cols(gsp[...], uu[:, columns])
+        return 0
+
+    lax.fori_loop(0, WIDTH // 256, spread_back, 0)
+    gni[0:GROUP] += class_in[0:GROUP]
+    gni[half : half + GROUP] += class_in[GROUP:]
+
+    def norm_one_back(step, sums):
+        rows = pl.ds(pl.multiple_of(step * STEP, STEP), STEP)
+        _, unit, factor = layer_norm(x[rows, :].astype(F32), ln1_gain[...], ln1_bias[...])
+        parts = []
+        for part in range(2):
+            source = pl.ds(pl.multiple_of(part * half + step * (STEP // 2), 16), STEP // 2)
+            parts.append(gni[source, :].reshape(STEP // 16, GROUP, WIDTH))
+        grad_out = jnp.stack(parts, 1).reshape(STEP, WIDTH)
+        grad_in, gain_part, bias_part = norm_back(grad_out, unit, factor, ln1_gain[...])
+        grad_images[rows, :] = grad_in
+        return (sums[0] + gain_part[None], sums[1] + bias_part[None])
+
+    zero = jnp.zeros((1, WIDTH), F32)
+    g_ln1_gain, g_ln1_bias = lax.fori_loop(0, rows_all // STEP, norm_one_back, (zero, zero))
+    grad_images[0:images_here] += grad_middle
+
+    vectors = (
+        g_ln1_gain, g_ln1_bias, g_ln2_gain[None], g_ln2_bias[None], g_post_gain[None], g_post_bias[None],
+        g_text_gain[None], g_text_bias[None],
+    )
+    for index, vector in enumerate(vectors):
+        vec_z[z, index : index + 1, 0 : vector.shape[1]] = vector
+        vec_z[z, index : index + 1, WIDTH:] = g_fc1_bias[:, index * 384 : index * 384 + 384]
+    lane = lax.broadcasted_iota(jnp.int32, (2, 256), 1)
+    row = lax.broadcasted_iota(jnp.int32, (2, 256), 0)
+    vec_z[z, 6:8, EMBED:WIDTH] = jnp.where((lane == 0) & (row == 0), loss_part, 0.0) + jnp.where(
+        (lane == 0) & (row == 1), scale_part, 0.0
+    )
+    vec_line = to_line(lambda peer: vec_z.at[z], vec_z.at[z])
+
+    own_rf.wait()
+    for copy, is_keys, mine_keys in rf_copies:
+        copy.wait()
+    finish(co_copies)
+    columns_in = co_in[...].reshape(plane_images, 1024)
+    lane = lax.broadcasted_iota(jnp.int32, (planes * block_lanes, 128), 1)
+    for tile in range(5):
+        right = columns_in[:, tile * 128 : tile * 128 + 128]
+        got = dot_cols(rf_in[2 * tile].reshape(plane_images, planes * block_lanes), right)
+        if 2 * tile + 1 < heads_here:
+            other = dot_cols(rf_in[2 * tile + 1].reshape(plane_images, planes * block_lanes), right)
+            got = jnp.where(lane < HDIM, got, other)
+        ps_send[:, :, tile * 128 : tile * 128 + 128] = got.astype(BF16).reshape(planes, block_lanes, 128)
+    finish(ro_copies)
+    got = dot_cols(ro_in[0].reshape(plane_images, planes * block_lanes), columns_in[:, 640:896])
+    ps_send[:, :, 640:896] = got.astype(BF16).reshape(planes, block_lanes, 256)
+    got = dot_cols(ro_in[1].reshape(plane_images, planes * block_lanes), columns_in[:, 896:1024])
+    ps_send[:, :, 896:1024] = got.astype(BF16).reshape(planes, block_lanes, 128)
+    ps_copies = to_line(lambda peer: ps_send.at[peer], ps_recv.at[z])
+    ps_recv[z] = ps_send[z]
+    finish(tn_copies)
+    finish(te_copies)
+    got = dot_cols(
+        tn_in[...].reshape(plane_size * captions_here, planes * text_lanes),
+        te_in[...].reshape(plane_size * captions_here, 128),
+    )
+    pt_send[...] = got.astype(BF16).reshape(planes, text_lanes, 128)
+    pt_copies = to_line(lambda peer: pt_send.at[peer], pt_recv.at[z])
+    pt_recv[z] = pt_send[z]
+
+    finish(vec_line)
+    vec_p[slot] = jnp.sum(vec_z[...], 0)
+    vec_plane = to_plane(lambda peer: vec_p.at[slot], vec_p.at[slot])
+
+    finish(nm_plane)
+    all_rows = plane_images * planes
+    nm_rows = nm_full[...].reshape(all_rows, WIDTH)
+    my_columns = pl.ds(pl.multiple_of(dp * (HIDDEN // dp_size), 128), HIDDEN // dp_size)
+    my_rows = pl.ds(pl.multiple_of(rep * (HIDDEN // rep_size), 128), HIDDEN // rep_size)
+    hid_s[...] = matmul(nm_rows, fc1[:, my_columns]) + fc1_bias[:, my_columns]
+    hidden = matmul(nm_rows, fc1[:, my_rows]) + fc1_bias[:, my_rows]
+    act_s[...] = (hidden * jax.nn.sigmoid(1.702 * hidden)).astype(BF16)
+    source = lax.broadcasted_iota(jnp.int32, (WIDTH, 128), 0)
+    place = lax.broadcasted_iota(jnp.int32, (WIDTH, 128), 1)
+    chosen = jnp.where((source == place + rep * block_lanes) & (place < block_lanes), 1.0, 0.0).astype(BF16)
+    nm_sel[...] = matmul(nm_rows, chosen).astype(BF16)
+    finish(gb_plane)
+    gb_rows = gb_full[...].reshape(all_rows, WIDTH)
+    gate = jax.nn.sigmoid(1.702 * hid_s[...])
+    gh_s[...] = (
+        dot_rows(gb_rows, fc2[my_columns, :]) * (gate + 1.702 * hid_s[...] * gate * (1.0 - gate))
+    ).astype(BF16)
+    g_fc1[...] = dot_cols(nm_sel[...], gh_s[...])[0:block_lanes]
+    out_lanes = WIDTH // dp_size
+    source = lax.broadcasted_iota(jnp.int32, (WIDTH, 256), 0)
+    place = lax.broadcasted_iota(jnp.int32, (WIDTH, 256), 1)
+    chosen = jnp.where((source == place + dp * out_lanes) & (place < out_lanes), 1.0, 0.0).astype(BF16)
+    g_fc2[...] = dot_cols(matmul(gb_rows, chosen).astype(BF16), act_s[...])[0:out_lanes]
+
+    dense_attention(6, 12)
+    dense_out()
+    dense_ff()
+
+    finish(vec_plane)
+    g_vec[...] = jnp.sum(vec_p[...], 0)
+    finish(ps_copies)
+    summed = jnp.sum(ps_recv[...].astype(F32), 0)
+    g_qkv[...] = summed[:, 0:576]
+    g_out[...] = summed[:, 640:832]
+    g_ip[...] = summed[:, 896:1024]
+    finish(pt_copies)
+    g_tp[...] = jnp.sum(pt_recv[...].astype(F32), 0)
+    assert used[0] <= counter
+
+
+def fused_shards(
+    dp_size,
+    rep_size,
+    images,
+    qkv_weight,
+    out_weight,
+    fc1_weight,
+    fc1_bias,
+    fc2_weight,
+    ln1_gain,
+    ln1_bias,
+    ln2_gain,
+    ln2_bias,
+    post_gain,
+    post_bias,
+    image_proj,
+    text_feats,
+    text_gain,
+    text_bias,
+    text_proj,
+    log_scale,
+    caption_counts,
+    positives,
+):
+    images_here, patches, width = images.shape
+    captions_here = text_feats.shape[0]
+    sides = 2
+    planes = rep_size // sides
+    plane_size = dp_size * sides
+    rows_all = images_here * patches
+    heads_here = 3 * HEADS // dp_size
+    block = WIDTH // rep_size
+    text_block = EMBED // rep_size
+    spread = HEADS * images_here
+    line = planes * captions_here
+    total_images = plane_size * planes * images_here
+    copies = 192
+    vmem = pl.BlockSpec(memory_space=pltpu.VMEM)
+    hbm = pl.BlockSpec(memory_space=pl.ANY)
+
+    def f32(*shape):
+        return pltpu.VMEM(shape, F32)
+
+    def b16(*shape):
+        return pltpu.VMEM(shape, BF16)
+
+    out_shapes = (
+        ((rows_all, WIDTH), BF16),
+        ((rows_all, WIDTH), F32),
+        ((block, 3 * WIDTH // dp_size), F32),
+        ((block, WIDTH // dp_size), F32),
+        ((block, HIDDEN // dp_size), F32),
+        ((WIDTH // dp_size, HIDDEN // rep_size), F32),
+        ((block, EMBED // dp_size), F32),
+        ((captions_here, EMBED), F32),
+        ((text_block, EMBED // dp_size), F32),
+        ((8, 1152), F32),
+    )
+    scratch = [
+        b16(WIDTH, 3 * WIDTH), b16(WIDTH, WIDTH), b16(WIDTH, HIDDEN), b16(HIDDEN, WIDTH),
+        b16(WIDTH, EMBED), b16(EMBED, EMBED),
+        b16(rows_all, WIDTH), b16(rows_all, 2 * WIDTH), b16(rows_all, WIDTH), b16(rows_all, WIDTH),
+        f32(rows_all, WIDTH), b16(rows_all, WIDTH), f32(rows_all // 2, WIDTH), f32(rows_all, WIDTH),
+        f32(spread, rows_all), b16(spread, rows_all), b16(2 * spread, rows_all), b16(2 * spread, WIDTH),
+        f32(images_here, HIDDEN), f32(2, images_here, WIDTH),
+        b16(planes, captions_here, EMBED), f32(planes, captions_here, 128),
+        b16(plane_size, images_here, EMBED), f32(plane_size, images_here, 128),
+        f32(plane_size, 8, plane_size * images_here), f32(planes, 8, line),
+        f32(plane_size, images_here, EMBED), f32(plane_size, images_here, EMBED),
+        f32(planes, captions_here, EMBED), f32(planes, captions_here, EMBED),
+        b16(planes, plane_size, images_here, WIDTH), b16(planes, plane_size, images_here, WIDTH),
+        b16(sides, 3 * HEADS, images_here, planes * block),
+        b16(heads_here, plane_size, images_here, planes * block),
+        b16(sides, 2, images_here, planes * block), b16(2, plane_size, images_here, planes * block),
+        b16(sides, captions_here, planes * text_block), b16(plane_size, captions_here, planes * text_block),
+        b16(dp_size, images_here, 1024), b16(plane_size, images_here, 1024),
+        b16(dp_size, captions_here, 128), b16(plane_size, captions_here, 128),
+        b16(planes, block, 1024), b16(planes, block, 1024),
+        b16(planes, text_block, 128), b16(planes, text_block, 128),
+        f32(planes, 8, 1152), f32(plane_size, 8, 1152),
+        f32(total_images, HIDDEN // dp_size), b16(total_images, HIDDEN // rep_size),
+        b16(total_images, HIDDEN // dp_size), b16(total_images, 128),
+        pltpu.SemaphoreType.DMA((8,)), pltpu.SemaphoreType.DMA((copies,)), pltpu.SemaphoreType.DMA((copies,)),
+    ]
+    rows = images.transpose(1, 0, 2).reshape(rows_all, width)
+    results = pl.pallas_call(
+        functools.partial(
+            fused_kernel, (images_here, captions_here, planes, sides, dp_size), copies
+        ),
+        out_shape=tuple(jax.ShapeDtypeStruct(shape, kind) for shape, kind in out_shapes),
+        in_specs=[vmem] + [hbm] * 6 + [vmem] * 13,
+        out_specs=tuple(vmem for _ in out_shapes),
+        scratch_shapes=scratch,
+        compiler_params=pltpu.CompilerParams(
+            collective_id=1, has_side_effects=True, vmem_limit_bytes=60 * 2**20
+        ),
+        name="fused_block",
+    )(
+        rows, qkv_weight, out_weight, fc1_weight, fc2_weight, image_proj, text_proj,
+        fc1_bias.reshape(1, -1), ln1_gain.reshape(1, -1), ln1_bias.reshape(1, -1),
+        ln2_gain.reshape(1, -1), ln2_bias.reshape(1, -1), post_gain.reshape(1, -1),
+        post_bias.reshape(1, -1), text_feats, text_gain.reshape(1, -1), text_bias.reshape(1, -1),
+        log_scale.reshape(1, 1), caption_counts.reshape(1, -1), positives.reshape(1, -1),
+    )
+    block_out, grad_images, g_qkv, g_out, g_fc1, g_fc2, g_ip, g_text, g_tp, g_vec = results
+
+    def restore(values):
+        return values.reshape(patches, images_here, width).transpose(1, 0, 2)
+
+    image_total = images_here * dp_size * rep_size
+    return (
+        restore(block_out),
+        g_vec[6, EMBED] / image_total,
+        restore(grad_images),
+        g_qkv,
+        g_out,
+        g_fc1,
+        g_vec[:, WIDTH:].reshape(-1),
+        g_fc2.T,
+        g_vec[0, 0:WIDTH],
+        g_vec[1, 0:WIDTH],
+        g_vec[2, 0:WIDTH],
+        g_vec[3, 0:WIDTH],
+        g_vec[4, 0:WIDTH],
+        g_vec[5, 0:WIDTH],
+        g_ip,
+        g_text,
+        g_vec[6, 0:EMBED],
+        g_vec[7, 0:EMBED],
+        g_tp,
+        g_vec[7, EMBED : EMBED + 1],
+    )
+
+
 def solution(mesh):
+    dp_size, rep_size = mesh.shape["dp"], mesh.shape["rep"]
+    body = functools.partial(fused_shards, dp_size, rep_size) if fits(dp_size, rep_size) else shards
+
     return jax.shard_map(
-        shards,
+        body,
         mesh=mesh,
         in_specs=(
             P(("dp", "rep"), None, None),

time: 1160 us -> 120 us (0.10); the launches traced: 1140 us -> 119 us
  waiting for transfers between devices: 688 us -> 0 us
  blocking collectives: 152 us -> 0 us
  matrix products: 138 us -> 0 us
  Pallas kernels: 0 us -> 93.6 us
  local copies, waits for them, and re-layouts: 98.4 us -> 21.9 us
  other arithmetic: 46.2 us -> 0 us
  between operations: 20.3 us -> 3.15 us
    reduce_scatter x12 -> x0, waiting for transfers between devices: 559 us -> none  [the longest x1 84.4 us: shards(): lax.psum_scatter(logit_scale * matmul_left(columns, text_low), ('dp', 're...]
    dot_general x30 -> x0, matrix products: 138 us -> none  [the longest x8 43.8 us: matmul_left(): lax.dot_general(left, right, (((0,), (0,)), ((), ())), preferred_element_...]
    unnamed x17 -> x0, waiting for transfers between devices: 130 us -> none
    pallas_call x0 -> x1, Pallas kernels: none -> 93.6 us  [fused_shards(): pl.pallas_call(functools.partial(fused_kernel, (images_here, captions_her...]
    all_gather x1 -> x0, blocking collectives: 72.6 us -> none  [shards(): lax.all_gather(image_low, ('dp', 'rep'), axis=0, tiled=True)]
    psum x1 -> x0, blocking collectives: 41.8 us -> none  [shards(): total, scale_grad = lax.psum((total_part, scale_part), ('dp', 'rep'))]
    convert_element_type x8 -> x0, local copies, waits for them, and re-layouts: 40.1 us -> none  [the longest x2 22.1 us: shards(): grad_packed = jnp.stack([grad_query, grad_keys, grad_values], 2).reshape(...]
    unnamed x1 -> x0, blocking collectives: 37.4 us -> none
  transfers between devices with their start and end apart: 15 -> 0, of which waited for: 11 -> 0; matrix products, arithmetic and copies ran while one was open for 24% -> 0% of each run, Pallas kernels for 0% -> 0%
where the time goes in v1:
time: 120 us; the launch traced here: 119 us
  Pallas kernels  93.6 us (78%)
  local copies, waits for them, and re-layouts  21.9 us (18%)
  between operations  3.15 us (3%)
    pallas_call x1, Pallas kernels, fused_shards(): pl.pallas_call(functools.partial(fused_kernel, (images_here, captions_her...  93.6 us
    unnamed x25, local copies, waits for them, and re-layouts  8.5 us

profile of v1, /device:TPU:0, one launch (start us, length us, event | category | flops | bytes accessed | tf_op | source)
XLA Modules:
  0.0 118.6 jit_solution(424523394557383704)
XLA Ops:
  1.3 1.3 %reshape.92.refs_8_ = f32[1,768]{1,0:T(1,128)} reshape(f32[768]{0:T(1024)} %param.26) | data formatting | bytes 6144 | tf_op jit(solution)/shard_map/reshape | solution.py:943
  2.6 1.3 %reshape.93.refs_9_ = f32[1,768]{1,0:T(1,128)} reshape(f32[768]{0:T(1024)} %param.27) | data formatting | bytes 6144 | tf_op jit(solution)/shard_map/reshape | solution.py:943
  3.8 1.3 %reshape.94.refs_10_ = f32[1,768]{1,0:T(1,128)} reshape(f32[768]{0:T(1024)} %param.28) | data formatting | bytes 6144 | tf_op jit(solution)/shard_map/reshape | solution.py:944
  5.1 1.3 %reshape.95.refs_11_ = f32[1,768]{1,0:T(1,128)} reshape(f32[768]{0:T(1024)} %param.29) | data formatting | bytes 6144 | tf_op jit(solution)/shard_map/reshape | solution.py:944
  6.4 1.3 %reshape.96.refs_12_ = f32[1,768]{1,0:T(1,128)} reshape(f32[768]{0:T(1024)} %param.30) | data formatting | bytes 6144 | tf_op jit(solution)/shard_map/reshape | solution.py:944
  7.6 1.3 %reshape.97.refs_13_ = f32[1,768]{1,0:T(1,128)} reshape(f32[768]{0:T(1024)} %param.31) | data formatting | bytes 6144 | tf_op jit(solution)/shard_map/reshape | solution.py:945
  8.9 93.6 %fused_block.1 = (bf16[800,768]{1,0:T(8,128)(2,1)}, f32[800,768]{1,0:T(8,128)}, f32[96,576]{1,0:T(8,128)}, f32[96,192]{1,0:T(8,128)}, f32[96,768]{1,0:T(8,128)},...) custom-call(bf16[800,768]{1,0:T(8,128)(2,1)} %bitcast.23, ...), custom_call_target="tpu_custom_call" | custom-call | tf_op jit(solution)/shard_map/fused_block/pallas_call | solution.py:929
  102.5 0.0 copy-start
  102.5 1.3 %fusion = (f32[1,1]{1,0:T(1,128)}, f32[1,1]{1,0:T(1,128)}) fusion(f32[8,1152]{1,0:T(8,128)} %get-tuple-element.31), kind=kLoop, calls=%fused_computation.6 | loop fusion | bytes 16 | tf_op jit(solution)/shard_map/slice | solution.py:974
  104.5 1.4 %fusion.1 = (f32[1,512]{1,0:T(1,128)}, f32[1,512]{1,0:T(1,128)}) fusion(f32[8,1152]{1,0:T(8,128)} %get-tuple-element.31), kind=kLoop, calls=%fused_computation.7 | loop fusion | bytes 8192 | tf_op jit(solution)/shard_map/slice | solution.py:972
  105.9 0.7 slice.34
  106.6 1.7 %slice_reduce_fusion = (f32[768]{0:T(1024)}, f32[768]{0:T(1024)}, f32[768]{0:T(1024)}, f32[768]{0:T(1024)}, f32[768]{0:T(1024)}, /*index=5*/f32[768]{0:T(1024)}) fusion(f32[8,1152]{1,0:T(8,128)} %get-tuple-element.31), kind=kLoop, calls=%fused_computation | loop fusion | bytes 36864 | tf_op jit(solution)/shard_map/slice | solution.py:968
  108.3 0.6 reshape.105
  108.9 2.4 %copy.50 = bf16[16,50,768]{2,0,1:T(8,128)(2,1)} copy(bf16[16,50,768]{2,0,1:T(8,128)(2,1)} %bitcast.22) | data formatting | bytes 2457600
  111.3 0.0 copy-done
  111.3 0.0 copy-start.1
  111.4 1.4 %copy.51 = f32[16,50,768]{2,0,1:T(8,128)} copy(f32[16,50,768]{2,0,1:T(8,128)S(1)} %bitcast.21) | data formatting | bytes 4915200
  112.8 0.7 copy.52
  113.5 0.6 copy.53
  114.2 0.7 copy.54
  114.9 0.7 copy.55
  115.6 0.6 copy.56
  116.2 0.6 copy.57
  116.9 0.6 copy.58
  (13 shorter events, 0.0 us)
Async XLA Ops:
  102.5 8.8 %copy-start = (f32[800,768]{1,0:T(8,128)S(1)}, f32[800,768]{1,0:T(8,128)}, u32[]{:S(2)}) copy-start(f32[800,768]{1,0:T(8,128)} %get-tuple-element.32) | copy-start | bytes 7372804
  111.3 1.5 %copy-start.3 = (f32[96,576]{1,0:T(8,128)S(1)}, f32[96,576]{1,0:T(8,128)}, u32[]{:S(2)}) copy-start(f32[96,576]{1,0:T(8,128)} %get-tuple-element.73) | copy-start | bytes 663556
  111.3 2.2 %copy-start.5 = (f32[96,192]{1,0:T(8,128)S(1)}, f32[96,192]{1,0:T(8,128)}, u32[]{:S(2)}) copy-start(f32[96,192]{1,0:T(8,128)} %get-tuple-element.74) | copy-start | bytes 221188
  111.3 2.8 %copy-start.2 = (f32[96,768]{1,0:T(8,128)S(1)}, f32[96,768]{1,0:T(8,128)}, u32[]{:S(2)}) copy-start(f32[96,768]{1,0:T(8,128)} %get-tuple-element.75) | copy-start | bytes 884740
  111.3 3.5 %copy-start.1 = (f32[192,384]{1,0:T(8,128)S(1)}, f32[192,384]{1,0:T(8,128)}, u32[]{:S(2)}) copy-start(f32[192,384]{1,0:T(8,128)} %get-tuple-element.36) | copy-start | bytes 884740
  111.3 4.2 %copy-start.6 = (f32[96,128]{1,0:T(8,128)S(1)}, f32[96,128]{1,0:T(8,128)}, u32[]{:S(2)}) copy-start(f32[96,128]{1,0:T(8,128)} %get-tuple-element.84) | copy-start | bytes 147460
  111.4 4.9 %copy-start.4 = (f32[48,512]{1,0:T(8,128)S(1)}, f32[48,512]{1,0:T(8,128)}, u32[]{:S(2)}) copy-start(f32[48,512]{1,0:T(8,128)} %get-tuple-element.85) | copy-start | bytes 294916
  111.4 5.5 %copy-start.7 = (f32[64,128]{1,0:T(8,128)S(1)}, f32[64,128]{1,0:T(8,128)}, u32[]{:S(2)}) copy-start(f32[64,128]{1,0:T(8,128)} %get-tuple-element.88) | copy-start | bytes 98308

commit v2 on v1

--- a/solution.py
+++ b/solution.py
@@ -338,19 +338,20 @@
 
 def fused_kernel(dims, counter, *refs):
     (
-        x, qkv_hbm, out_hbm, fc1_hbm, fc2_hbm, ip_hbm, tp_hbm, fc1_bias,
-        ln1_gain, ln1_bias, ln2_gain, ln2_bias, post_gain, post_bias,
-        text_feats, text_gain, text_bias, log_scale, caption_counts, positives,
-        block_out, grad_images, g_qkv, g_out, g_fc1, g_fc2, g_ip, g_text, g_tp, g_vec,
-        qkv, w_out, fc1, fc2, ip, tp,
-        ni, kv, qd, mixed, middle, nmd, ff_acc, gni,
+        x_hbm, qkv_hbm, out_hbm, fc1_hbm, fc2_hbm, ip_hbm, tp_hbm, fc1_bias_in,
+        ln1_gain_in, ln1_bias_in, ln2_gain_in, ln2_bias_in, post_gain_in, post_bias_in,
+        text_feats, text_gain_in, text_bias_in, log_scale_in, caption_counts, positives,
+        block_hbm, images_hbm, qkv_out, w_out_out, fc1_out, fc2_out, ip_out, text_out, tp_out, g_vec,
+        x, qkv, w_out, fc1, fc2, ip, tp,
+        ni, kv, qd, mixed, middle, nmd, block_out, grad_images,
+        g_qkv, g_out, g_fc1, g_fc2, g_ip, g_text, g_tp,
         attn, attn_low, gsp, uu,
         hid_c, small,
         t_all, pos_all, i_all, cnt_all, row_sum, col_sum,
         gi_send, gi_recv, gt_send, gt_recv,
-        nm_full, gb_full, rf_out, rf_in, ro_out, ro_in, tn_out, tn_in,
-        co_out, co_in, te_out, te_in, ps_send, ps_recv, pt_send, pt_recv,
-        vec_z, vec_p, hid_s, act_s, gh_s, nm_sel,
+        nm_full, gb_full, rf_out, rf_in, ro_out, ro_in, cn_out, cn_in, tn_out, tn_in,
+        ca_out, ca_in, co_out, co_in, te_out, te_in, pa_send, pa_recv, ps_send, ps_recv, pt_send, pt_recv,
+        vec_out, vec_in, vec_z, vec_all, hid_s, act_s, gh_s, nm_sel,
         local_sem, send_sem, recv_sem,
     ) = refs
     images_here, captions_here, planes, sides, dp_size = dims
@@ -363,6 +364,8 @@
     z = rep // sides
     side = lax.rem(rep, sides)
     slot = dp * sides + side
+    row_y = dp // 2
+    core = lax.rem(dp, 2)
     plane_images = plane_size * images_here
     line_captions = planes * captions_here
     image_total = plane_images * planes
@@ -370,6 +373,12 @@
     text_ratio = image_total / caption_total
 
     used = [0]
+    fc1_bias = fc1_bias_in[...].reshape(1, HIDDEN)
+    ln1_gain, ln1_bias, ln2_gain, ln2_bias, post_gain, post_bias = (
+        ref[...].reshape(1, WIDTH)
+        for ref in (ln1_gain_in, ln1_bias_in, ln2_gain_in, ln2_bias_in, post_gain_in, post_bias_in)
+    )
+    text_gain, text_bias = (ref[...].reshape(1, EMBED) for ref in (text_gain_in, text_bias_in))
 
     def plane_peer(step):
         peer = lax.rem(slot + step, plane_size)
@@ -379,39 +388,62 @@
         peer = lax.rem(z + step, planes)
         return peer, (dp, peer * sides + side)
 
-    def copy_to(source, target, device):
-        index = used[0]
-        used[0] += 1
+    def copy_to(source, target, device, sends, arrivals):
         return pltpu.make_async_remote_copy(
-            src_ref=source, dst_ref=target, send_sem=send_sem.at[index], recv_sem=recv_sem.at[index],
+            src_ref=source, dst_ref=target, send_sem=send_sem.at[sends], recv_sem=recv_sem.at[arrivals],
             device_id=device, device_id_type=MESH,
         )
 
-    def to_plane(source_of, target):
-        copies = []
-        for step in range(1, plane_size):
-            peer, device = plane_peer(step)
-            copies.append(copy_to(source_of(peer), target, device))
-        for copy in copies:
-            copy.start()
-        return copies
-
-    def to_line(source_of, target):
-        copies = []
-        for step in range(1, planes):
-            peer, device = line_peer(step)
-            copies.append(copy_to(source_of(peer), target, device))
-        for copy in copies:
-            copy.start()
-        return copies
-
-    def finish(copies):
-        for copy in copies:
-            copy.wait()
+    def take(count=1):
+        used[0] += count
+        return used[0] - count
+
+    def exchange(peers, source_of, target, whole):
+        index = take()
+        for peer, device in peers:
+            copy_to(source_of(peer), target, device, index, index).start()
+        return (whole, index)
+
+    def to_plane(source_of, target, whole):
+        return exchange([plane_peer(step) for step in range(1, plane_size)], source_of, target, whole)
+
+    def to_line(source_of, target, whole):
+        return exchange([line_peer(step) for step in range(1, planes)], source_of, target, whole)
+
+    def to_chips(buffer):
+        peers = []
+        for step in range(1, 2 * sides):
+            peer = lax.rem(row_y * sides + side + step, 2 * sides)
+            peers.append((peer, ((peer // sides) * 2 + core, z * sides + lax.rem(peer, sides))))
+        mine = buffer.at[:, row_y, core, side]
+        return exchange(peers, lambda peer: mine, mine, buffer.at[0 : planes - 1, 0])
+
+    def to_partner(buffer):
+        device = (row_y * 2 + 1 - core, rep)
+        mine = buffer.at[:, :, core]
+        return exchange([(0, device)], lambda peer: mine, mine, mine)
+
+    def finish(sent):
+        whole, index = sent
+        pltpu.make_async_copy(whole, whole, recv_sem.at[index]).wait()
+        pltpu.make_async_copy(whole, whole, send_sem.at[index]).wait()
+
+    others = plane_size - 1
+    lines = planes - 1
 
     loads = []
+
+    def put_out(source, target):
+        copy = pltpu.make_async_copy(source, target, local_sem.at[len(loads)])
+        loads.append(copy)
+        copy.start()
+        return copy
+
     for index, (source, target) in enumerate(
-        ((tp_hbm, tp), (qkv_hbm, qkv), (out_hbm, w_out), (fc1_hbm, fc1), (fc2_hbm, fc2), (ip_hbm, ip))
+        (
+            (tp_hbm, tp), (x_hbm, x), (qkv_hbm, qkv), (out_hbm, w_out), (fc1_hbm, fc1), (fc2_hbm, fc2),
+            (ip_hbm, ip),
+        )
     ):
         load = pltpu.make_async_copy(source, target, local_sem.at[index])
         load.start()
@@ -423,176 +455,151 @@
     for step in range(1, planes):
         pl.semaphore_signal(barrier, inc=1, device_id=line_peer(step)[1], device_id_type=MESH)
 
-    text_full, _, _ = layer_norm(text_feats[...].astype(F32), text_gain[...], text_bias[...])
+    text_full, _, _ = layer_norm(text_feats[...].astype(F32), text_gain, text_bias)
     text_norm = text_full.astype(BF16)
     loads[0].wait()
     text_unit, text_factor = unit_rows(matmul(text_norm, tp[...]))
     t_all[z] = text_unit.astype(BF16)
-    pos_rows = jnp.broadcast_to(positives[...].astype(F32), (128, captions_here))
+    pos_rows = jnp.broadcast_to(positives[...].reshape(1, captions_here).astype(F32), (128, captions_here))
     pos_all[z] = jnp.transpose(pos_rows)
-    cnt_rows = jnp.broadcast_to(caption_counts[...].astype(F32), (128, images_here))
+    cnt_rows = jnp.broadcast_to(caption_counts[...].reshape(1, images_here).astype(F32), (128, images_here))
     cnt_all[slot] = jnp.transpose(cnt_rows)
     pl.semaphore_wait(barrier, plane_size - 1 + planes - 1)
-    text_copies = to_line(lambda peer: t_all.at[z], t_all.at[z])
-    pos_copies = to_line(lambda peer: pos_all.at[z], pos_all.at[z])
-    cnt_copies = to_plane(lambda peer: cnt_all.at[slot], cnt_all.at[slot])
-
-    def norm_in(step, _):
-        rows = pl.ds(pl.multiple_of(step * STEP, STEP), STEP)
-        full, _, _ = layer_norm(x[rows, :].astype(F32), ln1_gain[...], ln1_bias[...])
+    text_copies = to_line(lambda peer: t_all.at[z], t_all.at[z], t_all.at[0:lines])
+    pos_copies = to_line(lambda peer: pos_all.at[z], pos_all.at[z], pos_all.at[0:lines])
+    cnt_copies = to_plane(lambda peer: cnt_all.at[slot], cnt_all.at[slot], cnt_all.at[0:others])
+    text_lanes = EMBED // rep_size
+    for to_side in range(sides):
+        tn_out[to_side] = pick_blocks(text_full, to_side, sides, text_lanes, planes).astype(BF16)
+    tn_copies = to_plane(lambda peer: tn_out.at[lax.rem(peer, sides)], tn_in.at[slot], tn_in.at[0:others])
+    tn_in[slot] = tn_out[side]
+
+    loads[1].wait()
+    for first in range(0, rows_all, STEP):
+        full = layer_norm(x[first : first + STEP, :].astype(F32), ln1_gain, ln1_bias)[0]
         full = full.reshape(STEP // 16, 2, GROUP, WIDTH)
         for part in range(2):
-            to = pl.ds(pl.multiple_of(part * half + step * (STEP // 2), 16), STEP // 2)
-            ni[to, :] = full[:, part].reshape(STEP // 2, WIDTH).astype(BF16)
-        return 0
-
-    lax.fori_loop(0, rows_all // STEP, norm_in, 0)
-
-    loads[1].wait()
-
-    def keys_values(step, _):
-        source = pl.ds(pl.multiple_of(WIDTH + step * 256, 256), 256)
-        to = pl.ds(pl.multiple_of(step * 256, 256), 256)
-        kv[:, to] = matmul(ni[...], qkv[:, source]).astype(BF16)
-        return 0
-
-    lax.fori_loop(0, 2 * WIDTH // 256, keys_values, 0)
+            to = part * half + first // 2
+            ni[to : to + STEP // 2, :] = full[:, part].reshape(STEP // 2, WIDTH).astype(BF16)
+
+    loads[2].wait()
+    for first in range(0, 2 * WIDTH, WIDTH):
+        kv[:, first : first + WIDTH] = matmul(ni[...], qkv[:, WIDTH + first : 2 * WIDTH + first]).astype(BF16)
 
     resid_c = x[0:images_here, :].astype(F32)
-    normed_c = layer_norm(resid_c, ln1_gain[...], ln1_bias[...])[0].astype(BF16)
+    normed_c = layer_norm(resid_c, ln1_gain, ln1_bias)[0].astype(BF16)
     query_c = matmul(normed_c, qkv[:, 0:WIDTH]).astype(BF16)
     query_spread = head_spread(query_c.astype(F32)).astype(BF16)
     scores = 0.125 * dot_rows(query_spread, kv[:, 0:WIDTH])
-    row_image = lax.rem(lax.broadcasted_iota(jnp.int32, scores.shape, 0), images_here)
+    row_image = lax.broadcasted_iota(jnp.int32, scores.shape, 0) & (images_here - 1)
     column = lax.broadcasted_iota(jnp.int32, scores.shape, 1)
-    column_image = jnp.where(column < half, 0, GROUP) + lax.rem(column, GROUP)
+    column_image = jnp.where(column < half, 0, GROUP) + (column & (GROUP - 1))
     scores = jnp.where(row_image == column_image, scores, -1e30)
     weights = jnp.exp(scores - jnp.max(scores, 1, keepdims=True))
     weights = weights * (1.0 / jnp.sum(weights, 1, keepdims=True))
     attn[...] = weights
     attn_low[...] = weights.astype(BF16)
     mixed_c = head_gather(matmul(attn_low[...], kv[:, WIDTH:]))
-    loads[2].wait()
+    block_lanes = WIDTH // rep_size
+    mixed_f, normed_f = mixed_c.astype(BF16).astype(F32), normed_c.astype(F32)
+    for to_side in range(sides):
+        ro_out[to_side, 0] = pick_blocks(mixed_f, to_side, sides, block_lanes, planes).astype(BF16)
+        ro_out[to_side, 1] = pick_blocks(normed_f, to_side, sides, block_lanes, planes).astype(BF16)
+    ro_copies = to_plane(
+        lambda peer: ro_out.at[lax.rem(peer, sides)], ro_in.at[:, slot], ro_in.at[:, 0:others]
+    )
+    ro_in[:, slot] = ro_out[side]
+    loads[3].wait()
     middle_c = resid_c + matmul(mixed_c.astype(BF16), w_out[...])
-    full, unit_two, factor_two = layer_norm(middle_c, ln2_gain[...], ln2_bias[...])
-    nm_full[z, slot] = full.astype(BF16)
-    nm_line = to_line(lambda peer: nm_full.at[z, slot], nm_full.at[z, slot])
-    loads[3].wait()
-    hid_c[...] = matmul(full.astype(BF16), fc1[...]) + fc1_bias[...]
+    full, unit_two, factor_two = layer_norm(middle_c, ln2_gain, ln2_bias)
+    nm_full[z, row_y, core, side] = full.astype(BF16)
+    nm_line = to_line(
+        lambda peer: nm_full.at[z, row_y, core, side], nm_full.at[z, row_y, core, side], nm_full.at[0:lines, 0, 0, 0]
+    )
+    loads[4].wait()
+    hid_c[...] = matmul(full.astype(BF16), fc1[...]) + fc1_bias
     act_c = (hid_c[...] * jax.nn.sigmoid(1.702 * hid_c[...])).astype(BF16)
-    loads[4].wait()
+    loads[5].wait()
     block_c = middle_c + matmul(act_c, fc2[...])
-    full, unit_post, factor_post = layer_norm(block_c, post_gain[...], post_bias[...])
+    full, unit_post, factor_post = layer_norm(block_c, post_gain, post_bias)
     class_norm = full.astype(BF16)
-    loads[5].wait()
+    loads[6].wait()
     image_unit, image_factor = unit_rows(matmul(class_norm, ip[...]))
     i_all[slot] = image_unit.astype(BF16)
-    image_copies = to_plane(lambda peer: i_all.at[slot], i_all.at[slot])
+    image_copies = to_plane(lambda peer: i_all.at[slot], i_all.at[slot], i_all.at[0:others])
     small[0] = unit_two
     small[1] = unit_post
 
     value_rows = matmul(attn_low[...], ni[...])
-    normed_cf = normed_c.astype(F32)
-    block_lanes = WIDTH // rep_size
-    text_lanes = EMBED // rep_size
     for to_side in range(sides):
         picked = pick_blocks(value_rows, to_side, sides, block_lanes, planes).astype(BF16)
-        rf_out[to_side, 2 * HEADS : 3 * HEADS] = picked.reshape(HEADS, images_here, planes * block_lanes)
-        picked = pick_blocks(normed_cf, to_side, sides, block_lanes, planes).astype(BF16)
-        rf_out[to_side, 0:HEADS] = jnp.broadcast_to(picked[None], (HEADS, images_here, planes * block_lanes))
-        ro_out[to_side, 0] = pick_blocks(mixed_c, to_side, sides, block_lanes, planes).astype(BF16)
-        ro_out[to_side, 1] = pick_blocks(full, to_side, sides, block_lanes, planes).astype(BF16)
-        tn_out[to_side] = pick_blocks(text_full, to_side, sides, text_lanes, planes).astype(BF16)
+        rf_out[to_side, HEADS:] = picked.reshape(HEADS, images_here, planes * block_lanes)
+        cn_out[to_side] = pick_blocks(full, to_side, sides, block_lanes, planes).astype(BF16)
+    cn_in[slot] = cn_out[side]
 
     heads_here = 3 * HEADS // dp_size
     bundle = heads_here // 3
     rf_copies = []
+    arrivals = take(3)
     for step in range(1, plane_size):
         peer, device = plane_peer(step)
         for part in range(3):
             first = (peer // sides) * heads_here + part * bundle
-            mine = dp * heads_here + part * bundle
             copy = copy_to(
-                rf_out.at[lax.rem(peer, sides), pl.ds(first, bundle)],
-                rf_in.at[pl.ds(part * bundle, bundle), slot], device,
+                rf_out.at[lax.rem(peer, sides), pl.ds(lax.rem(first + HEADS, 2 * HEADS), bundle)],
+                rf_in.at[pl.ds(part * bundle, bundle), slot], device, take(), arrivals + part,
             )
-            is_keys = (first >= HEADS) & (first < 2 * HEADS)
-            mine_keys = (mine >= HEADS) & (mine < 2 * HEADS)
-            rf_copies.append((copy, is_keys, mine_keys))
-
-    for copy, is_keys, _ in rf_copies:
-        pl.when(jnp.logical_not(is_keys))(copy.start)
-    ro_copies = to_plane(lambda peer: ro_out.at[lax.rem(peer, sides)], ro_in.at[:, slot])
-    tn_copies = to_plane(lambda peer: tn_out.at[lax.rem(peer, sides)], tn_in.at[slot])
+            rf_copies.append((copy, first))
+
+    def head_kind(first):
+        return first // HEADS
 
     def dense_query():
-        def piece(step, _):
-            columns = pl.ds(pl.multiple_of(step * 256, 256), 256)
-            qd[:, columns] = (0.125 * matmul(ni[...], qkv[:, columns]).astype(BF16).astype(F32)).astype(BF16)
-            return 0
-
-        lax.fori_loop(0, WIDTH // 256, piece, 0)
+        qd[...] = (0.125 * matmul(ni[...], qkv[:, 0:WIDTH]).astype(BF16).astype(F32)).astype(BF16)
 
     def dense_attention(first, last):
-        def piece(index, _):
-            part = index // (HEADS // 2)
-            pair = lax.rem(index, HEADS // 2)
-            rows = pl.ds(pl.multiple_of(part * half, 16), half)
-            lanes = pl.ds(pl.multiple_of(pair * 128, 128), 128)
-            value_lanes = pl.ds(pl.multiple_of(WIDTH + pair * 128, 128), 128)
+        lane = lax.broadcasted_iota(jnp.int32, (half, 128), 1)
+        apart = lax.broadcasted_iota(jnp.int32, (GROUP, half), 0) != (
+            lax.broadcasted_iota(jnp.int32, (GROUP, half), 1) & (GROUP - 1)
+        )
+        bias = jnp.where(apart, -1e30, 0.0)[None]
+        for index in range(first, last):
+            rows = slice((index % 2) * half, (index % 2) * half + half)
+            lanes = slice((index // 2) * 128, (index // 2) * 128 + 128)
             query = qd[rows, lanes]
             keys = kv[rows, lanes]
-            values = kv[rows, value_lanes]
-            lane = lax.broadcasted_iota(jnp.int32, (half, 128), 1)
-            row_of = lax.rem(lax.broadcasted_iota(jnp.int32, (half, half), 0), GROUP)
-            col_of = lax.rem(lax.broadcasted_iota(jnp.int32, (half, half), 1), GROUP)
-            same = row_of == col_of
+            values = kv[rows, WIDTH + lanes.start : WIDTH + lanes.stop]
             result = None
             for which in range(2):
                 own = (lane < HDIM) if which == 0 else (lane >= HDIM)
                 logits = dot_rows(jnp.where(own, query, jnp.zeros_like(query)), keys)
-                logits = jnp.where(same, logits, -1e30)
+                logits = (logits.reshape(half // GROUP, GROUP, half) + bias).reshape(half, half)
                 top = jnp.exp(logits - jnp.max(logits, 1, keepdims=True))
-                top = top * (1.0 / jnp.sum(top, 1, keepdims=True))
-                got = matmul(top.astype(BF16), values)
+                got = matmul(top.astype(BF16), values) * (1.0 / jnp.sum(top, 1, keepdims=True))
                 result = got if which == 0 else jnp.where(own, got, result)
             mixed[rows, lanes] = result.astype(BF16)
-            return 0
-
-        lax.fori_loop(first, last, piece, 0)
+
+    def join_groups(values, first):
+        parts = [
+            values[part * half + first // 2 : part * half + (first + STEP) // 2].reshape(STEP // 16, GROUP, WIDTH)
+            for part in range(2)
+        ]
+        return jnp.stack(parts, 1).reshape(STEP, WIDTH)
 
     def dense_out():
-        def piece(step, _):
-            parts = []
-            for part in range(2):
-                rows = pl.ds(pl.multiple_of(part * half + step * (STEP // 2), 16), STEP // 2)
-                parts.append(matmul(mixed[rows, :], w_out[...]).reshape(STEP // 16, GROUP, WIDTH))
-            joined = jnp.stack(parts, 1).reshape(STEP, WIDTH)
-            rows = pl.ds(pl.multiple_of(step * STEP, STEP), STEP)
-            value = x[rows, :].astype(F32) + joined
+        added = matmul(mixed[...], w_out[...])
+        for first in range(0, rows_all, STEP):
+            rows = slice(first, first + STEP)
+            value = x[rows, :].astype(F32) + join_groups(added, first)
             middle[rows, :] = value
-            nmd[rows, :] = layer_norm(value, ln2_gain[...], ln2_bias[...])[0].astype(BF16)
-            return 0
-
-        lax.fori_loop(0, rows_all // STEP, piece, 0)
-
-    def dense_ff():
-        def outer(part, _):
-            rows = pl.ds(pl.multiple_of(part * half, 16), half)
-            ff_acc[...] = middle[rows, :]
-
-            def inner(step, _):
-                columns = pl.ds(pl.multiple_of(step * 768, 768), 768)
-                hidden = matmul(nmd[rows, :], fc1[:, columns]) + fc1_bias[:, columns]
-                act = (hidden * jax.nn.sigmoid(1.702 * hidden)).astype(BF16)
-                ff_acc[...] += matmul(act, fc2[columns, :])
-                return 0
-
-            lax.fori_loop(0, HIDDEN // 768, inner, 0)
-            block_out[rows, :] = ff_acc[...].astype(BF16)
-            return 0
-
-        lax.fori_loop(0, 2, outer, 0)
+            nmd[rows, :] = layer_norm(value, ln2_gain, ln2_bias)[0].astype(BF16)
+
+    def dense_ff(part):
+        rows = slice(part * half, (part + 1) * half)
+        hidden = matmul(nmd[rows, :], fc1[...]) + fc1_bias
+        act = (hidden * jax.nn.sigmoid(1.702 * hidden)).astype(BF16)
+        block_out[rows, :] = (middle[rows, :] + matmul(act, fc2[...])).astype(BF16)
+        return put_out(block_out.at[rows], block_hbm.at[rows])
 
     dense_query()
 
@@ -600,7 +607,7 @@
     finish(pos_copies)
     finish(cnt_copies)
     finish(image_copies)
-    scale = jnp.exp(log_scale[...])
+    scale = jnp.exp(log_scale_in[...].reshape(1, 1))
     images_low = i_all[...].reshape(plane_images, EMBED)
     texts_low = t_all[...].reshape(line_captions, EMBED)
     logits = scale * dot_rows(images_low, texts_low)
@@ -618,14 +625,13 @@
     counts = jnp.transpose(cnt_all[...].reshape(plane_images, 128))[0:1, :]
     row_sum[slot] = jnp.broadcast_to(jnp.sum(jnp.exp(logits_t), 0, keepdims=True), (8, plane_images))
     col_sum[z] = jnp.broadcast_to(jnp.sum(jnp.exp(logits), 0, keepdims=True), (8, line_captions))
-    sum_copies = to_plane(lambda peer: row_sum.at[slot], row_sum.at[slot])
-    sum_copies += to_line(lambda peer: col_sum.at[z], col_sum.at[z])
-
-    finish(nm_line)
-    nm_plane = to_plane(lambda peer: nm_full.at[:, slot], nm_full.at[:, slot])
-    dense_attention(0, 3)
-
-    finish(sum_copies)
+    row_copies = to_plane(lambda peer: row_sum.at[slot], row_sum.at[slot], row_sum.at[0:others])
+    col_copies = to_line(lambda peer: col_sum.at[z], col_sum.at[z], col_sum.at[0:lines])
+
+    dense_attention(0, 6)
+
+    finish(row_copies)
+    finish(col_copies)
     row_lse = jnp.log(jnp.sum(row_sum[...], 0)[0:1])
     col_lse = jnp.log(jnp.sum(col_sum[...], 0)[0:1])
     grad_cols = (0.5 * text_ratio * (jnp.exp(logits - col_lse) - match)).astype(BF16)
@@ -634,37 +640,54 @@
         0.5 * text_ratio
     ) * (jnp.sum(col_lse) / planes - jnp.sum(match * logits))
     scale_part = jnp.sum(grad_cols.astype(F32) * logits) + jnp.sum(grad_rows_t.astype(F32) * logits_t)
-    gi_send[...] = (scale * (dot_cols(grad_rows_t, texts_low) + matmul(grad_cols, texts_low))).reshape(
-        plane_size, images_here, EMBED
-    )
-    gi_copies = to_plane(lambda peer: gi_send.at[peer], gi_recv.at[slot])
+    gi_send[...] = (
+        (scale * (dot_cols(grad_rows_t, texts_low) + matmul(grad_cols, texts_low)))
+        .astype(BF16)
+        .reshape(plane_size, images_here, EMBED)
+    )
+    gi_copies = to_plane(lambda peer: gi_send.at[peer], gi_recv.at[slot], gi_recv.at[0:others])
     gi_recv[slot] = gi_send[slot]
-    gt_send[...] = (scale * (dot_cols(grad_cols, images_low) + matmul(grad_rows_t, images_low))).reshape(
-        planes, captions_here, EMBED
-    )
-    gt_copies = to_line(lambda peer: gt_send.at[peer], gt_recv.at[z])
+    gt_send[...] = (
+        (scale * (dot_cols(grad_cols, images_low) + matmul(grad_rows_t, images_low)))
+        .astype(BF16)
+        .reshape(planes, captions_here, EMBED)
+    )
+    gt_copies = to_line(lambda peer: gt_send.at[peer], gt_recv.at[z], gt_recv.at[0:lines])
     gt_recv[z] = gt_send[z]
 
-    dense_attention(3, 6)
+    dense_attention(6, 12)
 
     finish(gi_copies)
-    grad_embed = unit_back(jnp.sum(gi_recv[...], 0), image_unit, image_factor).astype(BF16)
+    cn_copies = to_plane(lambda peer: cn_out.at[lax.rem(peer, sides)], cn_in.at[slot], cn_in.at[0:others])
+    for copy, first in rf_copies:
+        pl.when(head_kind(first) == 2)(copy.start)
+    grad_embed = unit_back(jnp.sum(gi_recv[...].astype(F32), 0), image_unit, image_factor).astype(BF16)
     grad_class, g_post_gain, g_post_bias = norm_back(
-        dot_rows(grad_embed, ip[...]), small[1], factor_post, post_gain[...]
+        dot_rows(grad_embed, ip[...]), small[1], factor_post, post_gain
     )
     gb_low = grad_class.astype(BF16)
-    gb_full[z, slot] = gb_low
-    gb_line = to_line(lambda peer: gb_full.at[z, slot], gb_full.at[z, slot])
+    gb_full[z, row_y, core, side] = gb_low
+    gb_line = to_line(
+        lambda peer: gb_full.at[z, row_y, core, side], gb_full.at[z, row_y, core, side], gb_full.at[0:lines, 0, 0, 0]
+    )
     gate = jax.nn.sigmoid(1.702 * hid_c[...])
     grad_hidden = (
         dot_rows(gb_low, fc2[...]) * (gate + 1.702 * hid_c[...] * gate * (1.0 - gate))
     ).astype(BF16)
     g_fc1_bias = jnp.sum(grad_hidden.astype(F32), 0, keepdims=True)
     grad_two, g_ln2_gain, g_ln2_bias = norm_back(
-        dot_rows(grad_hidden, fc1[...]), small[0], factor_two, ln2_gain[...]
+        dot_rows(grad_hidden, fc1[...]), small[0], factor_two, ln2_gain
     )
     grad_middle = grad_class + grad_two
     grad_middle_low = grad_middle.astype(BF16)
+    m_plain = grad_middle_low.astype(F32)
+    m_shift = lane_shift(m_plain, 64)
+    cuts = (m_plain[:, 0:192], m_shift[:, 128:320], m_plain[:, 384:576], m_shift[:, 512:704])
+    for to_dp, source in enumerate(cuts):
+        ca_out[to_dp, :, 0:192] = source.astype(BF16)
+        ca_out[to_dp, :, 256:384] = grad_embed[:, to_dp * 128 : to_dp * 128 + 128]
+    ca_copies = to_plane(lambda peer: ca_out.at[peer // sides], ca_in.at[slot], ca_in.at[0:others])
+    ca_in[slot] = ca_out[dp]
     grad_mixed = dot_rows(grad_middle_low, w_out[...]).astype(BF16)
     mixed_spread = head_spread(grad_mixed.astype(F32)).astype(BF16)
     grad_attn = dot_rows(mixed_spread, kv[:, WIDTH:])
@@ -678,15 +701,13 @@
     key_rows = matmul(score_low, ni[...])
     for to_side in range(sides):
         picked = pick_blocks(key_rows, to_side, sides, block_lanes, planes).astype(BF16)
-        rf_out[to_side, HEADS : 2 * HEADS] = picked.reshape(HEADS, images_here, planes * block_lanes)
+        rf_out[to_side, 0:HEADS] = picked.reshape(HEADS, images_here, planes * block_lanes)
 
     grad_q = grad_query.astype(F32)
     query_f = query_c.astype(F32)
     grad_v = grad_mixed.astype(F32)
     lane = lax.broadcasted_iota(jnp.int32, (images_here, 128), 1)
     q_shift, k_shift, v_shift = lane_shift(grad_q, 64), lane_shift(query_f, -64), lane_shift(grad_v, 64)
-    m_shift = lane_shift(grad_middle_low.astype(F32), 64)
-    m_plain = grad_middle_low.astype(F32)
     co_out[0, :, 0:576] = grad_q[:, 0:576].astype(BF16)
     co_out[1, :, 0:128] = q_shift[:, 512:640].astype(BF16)
     co_out[1, :, 128:256] = jnp.where(lane < 64, q_shift[:, 640:768], k_shift[:, 0:128]).astype(BF16)
@@ -694,98 +715,109 @@
     co_out[2, :, 0:384] = query_f[:, 384:768].astype(BF16)
     co_out[2, :, 384:576] = grad_v[:, 0:192].astype(BF16)
     co_out[3, :, 0:576] = v_shift[:, 128:704].astype(BF16)
-    for to_dp, source in enumerate((m_plain[:, 0:192], m_shift[:, 128:320], m_plain[:, 384:576], m_shift[:, 512:704])):
-        co_out[to_dp, :, 640:832] = source.astype(BF16)
-        co_out[to_dp, :, 896:1024] = grad_embed[:, to_dp * 128 : to_dp * 128 + 128]
-    co_copies = to_plane(lambda peer: co_out.at[peer // sides], co_in.at[slot])
-    for copy, is_keys, _ in rf_copies:
-        pl.when(is_keys)(copy.start)
-    own_rf = pltpu.make_async_copy(
-        rf_out.at[side, pl.ds(dp * heads_here, heads_here)], rf_in.at[:, slot], local_sem.at[6]
-    )
-    own_rf.start()
+    co_copies = to_plane(lambda peer: co_out.at[peer // sides], co_in.at[slot], co_in.at[0:others])
+    for copy, first in rf_copies:
+        pl.when(head_kind(first) == 1)(copy.start)
     co_in[slot] = co_out[dp]
-    ro_in[:, slot] = ro_out[side]
-    tn_in[slot] = tn_out[side]
+    for part in range(3):
+        mine = dp * heads_here + part * bundle
+
+        def keep(part=part, mine=mine):
+            own = rf_out[side, pl.ds(lax.rem(mine + HEADS, 2 * HEADS), bundle)]
+            rf_in[part * bundle : (part + 1) * bundle, slot] = own
+
+        pl.when(head_kind(mine) > 0)(keep)
+
+    rows_here = planes * block_lanes
+    finish(ro_copies)
+    finish(cn_copies)
+    finish(ca_copies)
+    columns_in = ca_in[...].reshape(plane_images, 384)
+    got = dot_cols(ro_in[0].reshape(plane_images, rows_here), columns_in[:, 0:256])
+    pa_send[:, :, 0:256] = got.astype(BF16).reshape(planes, block_lanes, 256)
+    got = dot_cols(cn_in[...].reshape(plane_images, rows_here), columns_in[:, 256:384])
+    pa_send[:, :, 256:384] = got.astype(BF16).reshape(planes, block_lanes, 128)
+    pa_copies = to_line(lambda peer: pa_send.at[peer], pa_recv.at[z], pa_recv.at[0:lines])
+    pa_recv[z] = pa_send[z]
 
     finish(gt_copies)
-    grad_text = unit_back(jnp.sum(gt_recv[...], 0), text_unit, text_factor).astype(BF16)
+    grad_text = unit_back(jnp.sum(gt_recv[...].astype(F32), 0), text_unit, text_factor).astype(BF16)
     for to_dp in range(dp_size):
         te_out[to_dp] = grad_text[:, to_dp * 128 : to_dp * 128 + 128]
-    te_copies = to_plane(lambda peer: te_out.at[peer // sides], te_in.at[slot])
+    te_copies = to_plane(lambda peer: te_out.at[peer // sides], te_in.at[slot], te_in.at[0:others])
     te_in[slot] = te_out[dp]
-    _, unit_text, factor_text = layer_norm(text_feats[...].astype(F32), text_gain[...], text_bias[...])
+    _, unit_text, factor_text = layer_norm(text_feats[...].astype(F32), text_gain, text_bias)
     g_feats, g_text_gain, g_text_bias = norm_back(
-        dot_rows(grad_text, tp[...]), unit_text, factor_text, text_gain[...]
+        dot_rows(grad_text, tp[...]), unit_text, factor_text, text_gain
     )
     g_text[...] = g_feats
 
+    finish(nm_line)
+    nm_chips = to_chips(nm_full)
     finish(gb_line)
-    gb_plane = to_plane(lambda peer: gb_full.at[:, slot], gb_full.at[:, slot])
+    gb_chips = to_chips(gb_full)
 
     uu[0 : HEADS * images_here] = dot_rows(query_spread, qkv[:, WIDTH : 2 * WIDTH]).astype(BF16)
     uu[HEADS * images_here :] = dot_rows(mixed_spread, qkv[:, 2 * WIDTH :]).astype(BF16)
     class_in = dot_rows(grad_query, qkv[:, 0:WIDTH])
 
-    def spread_back(step, _):
-        columns = pl.ds(pl.multiple_of(step * 256, 256), 256)
-        gni[:, columns] = dot_cols(gsp[...], uu[:, columns])
-        return 0
-
-    lax.fori_loop(0, WIDTH // 256, spread_back, 0)
-    gni[0:GROUP] += class_in[0:GROUP]
-    gni[half : half + GROUP] += class_in[GROUP:]
-
-    def norm_one_back(step, sums):
-        rows = pl.ds(pl.multiple_of(step * STEP, STEP), STEP)
-        _, unit, factor = layer_norm(x[rows, :].astype(F32), ln1_gain[...], ln1_bias[...])
-        parts = []
-        for part in range(2):
-            source = pl.ds(pl.multiple_of(part * half + step * (STEP // 2), 16), STEP // 2)
-            parts.append(gni[source, :].reshape(STEP // 16, GROUP, WIDTH))
-        grad_out = jnp.stack(parts, 1).reshape(STEP, WIDTH)
-        grad_in, gain_part, bias_part = norm_back(grad_out, unit, factor, ln1_gain[...])
+    spread = dot_cols(gsp[...], uu[...])
+    g_ln1_gain = jnp.zeros((1, WIDTH), F32)
+    g_ln1_bias = jnp.zeros((1, WIDTH), F32)
+    for first in range(0, rows_all, STEP):
+        rows = slice(first, first + STEP)
+        _, unit, factor = layer_norm(x[rows, :].astype(F32), ln1_gain, ln1_bias)
+        grad_out = join_groups(spread, first)
+        if first == 0:
+            grad_out = jnp.concatenate([grad_out[0:images_here] + class_in, grad_out[images_here:]], 0)
+        grad_in, gain_part, bias_part = norm_back(grad_out, unit, factor, ln1_gain)
         grad_images[rows, :] = grad_in
-        return (sums[0] + gain_part[None], sums[1] + bias_part[None])
-
-    zero = jnp.zeros((1, WIDTH), F32)
-    g_ln1_gain, g_ln1_bias = lax.fori_loop(0, rows_all // STEP, norm_one_back, (zero, zero))
+        g_ln1_gain += gain_part[None]
+        g_ln1_bias += bias_part[None]
     grad_images[0:images_here] += grad_middle
+    outs = [put_out(grad_images, images_hbm), put_out(g_text, text_out)]
 
     vectors = (
         g_ln1_gain, g_ln1_bias, g_ln2_gain[None], g_ln2_bias[None], g_post_gain[None], g_post_bias[None],
         g_text_gain[None], g_text_bias[None],
     )
     for index, vector in enumerate(vectors):
-        vec_z[z, index : index + 1, 0 : vector.shape[1]] = vector
-        vec_z[z, index : index + 1, WIDTH:] = g_fc1_bias[:, index * 384 : index * 384 + 384]
-    lane = lax.broadcasted_iota(jnp.int32, (2, 256), 1)
-    row = lax.broadcasted_iota(jnp.int32, (2, 256), 0)
-    vec_z[z, 6:8, EMBED:WIDTH] = jnp.where((lane == 0) & (row == 0), loss_part, 0.0) + jnp.where(
-        (lane == 0) & (row == 1), scale_part, 0.0
-    )
-    vec_line = to_line(lambda peer: vec_z.at[z], vec_z.at[z])
-
-    own_rf.wait()
-    for copy, is_keys, mine_keys in rf_copies:
-        copy.wait()
+        vec_out[index, :, 0 : vector.shape[1]] = vector
+        vec_out[index, :, WIDTH:] = g_fc1_bias[:, index * 384 : index * 384 + 384]
+    first_lane = lax.broadcasted_iota(jnp.int32, (1, 256), 1) == 0
+    vec_out[6, :, EMBED:WIDTH] = jnp.where(first_lane, loss_part, 0.0)
+    vec_out[7, :, EMBED:WIDTH] = jnp.where(first_lane, scale_part, 0.0)
+    vec_plane = to_plane(lambda peer: vec_out.at[peer], vec_in.at[slot], vec_in.at[0:others])
+    vec_in[slot] = vec_out[slot]
+
+    for part in range(3):
+        mine = dp * heads_here + part * bundle
+        here = rf_in.at[part * bundle : (part + 1) * bundle, 0:others]
+        pl.when(head_kind(mine) > 0)(pltpu.make_async_copy(here, here, recv_sem.at[arrivals + part]).wait)
+
+        def repeat(part=part):
+            rf_in[part * bundle : (part + 1) * bundle] = jnp.broadcast_to(
+                ro_in[1][None], (bundle, plane_size, images_here, rows_here)
+            )
+
+        pl.when(head_kind(mine) == 0)(repeat)
     finish(co_copies)
-    columns_in = co_in[...].reshape(plane_images, 1024)
-    lane = lax.broadcasted_iota(jnp.int32, (planes * block_lanes, 128), 1)
+    columns_in = co_in[...].reshape(plane_images, 640)
+    lane = lax.broadcasted_iota(jnp.int32, (rows_here, 128), 1)
     for tile in range(5):
         right = columns_in[:, tile * 128 : tile * 128 + 128]
-        got = dot_cols(rf_in[2 * tile].reshape(plane_images, planes * block_lanes), right)
+        got = dot_cols(rf_in[2 * tile].reshape(plane_images, rows_here), right)
         if 2 * tile + 1 < heads_here:
-            other = dot_cols(rf_in[2 * tile + 1].reshape(plane_images, planes * block_lanes), right)
+            other = dot_cols(rf_in[2 * tile + 1].reshape(plane_images, rows_here), right)
             got = jnp.where(lane < HDIM, got, other)
-        ps_send[:, :, tile * 128 : tile * 128 + 128] = got.astype(BF16).reshape(planes, block_lanes, 128)
-    finish(ro_copies)
-    got = dot_cols(ro_in[0].reshape(plane_images, planes * block_lanes), columns_in[:, 640:896])
-    ps_send[:, :, 640:896] = got.astype(BF16).reshape(planes, block_lanes, 256)
-    got = dot_cols(ro_in[1].reshape(plane_images, planes * block_lanes), columns_in[:, 896:1024])
-    ps_send[:, :, 896:1024] = got.astype(BF16).reshape(planes, block_lanes, 128)
-    ps_copies = to_line(lambda peer: ps_send.at[peer], ps_recv.at[z])
+        width = min(128, 576 - tile * 128)
+        ps_send[:, :, tile * 128 : tile * 128 + width] = (
+            got[:, 0:width].astype(BF16).reshape(planes, block_lanes, width)
+        )
+    ps_copies = to_line(lambda peer: ps_send.at[peer], ps_recv.at[z], ps_recv.at[0:lines])
     ps_recv[z] = ps_send[z]
+    for copy, first in rf_copies:
+        pl.when(head_kind(first) > 0)(copy.wait_send)
     finish(tn_copies)
     finish(te_copies)
     got = dot_cols(
@@ -793,26 +825,30 @@
         te_in[...].reshape(plane_size * captions_here, 128),
     )
     pt_send[...] = got.astype(BF16).reshape(planes, text_lanes, 128)
-    pt_copies = to_line(lambda peer: pt_send.at[peer], pt_recv.at[z])
+    pt_copies = to_line(lambda peer: pt_send.at[peer], pt_recv.at[z], pt_recv.at[0:lines])
     pt_recv[z] = pt_send[z]
 
-    finish(vec_line)
-    vec_p[slot] = jnp.sum(vec_z[...], 0)
-    vec_plane = to_plane(lambda peer: vec_p.at[slot], vec_p.at[slot])
-
-    finish(nm_plane)
+    finish(vec_plane)
+    vec_z[z] = jnp.sum(vec_in[...], 0)
+    vec_line = to_line(lambda peer: vec_z.at[z], vec_z.at[z], vec_z.at[0:lines])
+    finish(nm_chips)
+    nm_partner = to_partner(nm_full)
+
+    finish(gb_chips)
+    gb_partner = to_partner(gb_full)
+    finish(nm_partner)
     all_rows = plane_images * planes
     nm_rows = nm_full[...].reshape(all_rows, WIDTH)
     my_columns = pl.ds(pl.multiple_of(dp * (HIDDEN // dp_size), 128), HIDDEN // dp_size)
     my_rows = pl.ds(pl.multiple_of(rep * (HIDDEN // rep_size), 128), HIDDEN // rep_size)
-    hid_s[...] = matmul(nm_rows, fc1[:, my_columns]) + fc1_bias[:, my_columns]
-    hidden = matmul(nm_rows, fc1[:, my_rows]) + fc1_bias[:, my_rows]
+    hid_s[...] = matmul(nm_rows, fc1[:, my_columns]) + fc1_bias_in[my_columns].reshape(1, HIDDEN // dp_size)
+    hidden = matmul(nm_rows, fc1[:, my_rows]) + fc1_bias_in[my_rows].reshape(1, HIDDEN // rep_size)
     act_s[...] = (hidden * jax.nn.sigmoid(1.702 * hidden)).astype(BF16)
     source = lax.broadcasted_iota(jnp.int32, (WIDTH, 128), 0)
     place = lax.broadcasted_iota(jnp.int32, (WIDTH, 128), 1)
     chosen = jnp.where((source == place + rep * block_lanes) & (place < block_lanes), 1.0, 0.0).astype(BF16)
     nm_sel[...] = matmul(nm_rows, chosen).astype(BF16)
-    finish(gb_plane)
+    finish(gb_partner)
     gb_rows = gb_full[...].reshape(all_rows, WIDTH)
     gate = jax.nn.sigmoid(1.702 * hid_s[...])
     gh_s[...] = (
@@ -825,20 +861,59 @@
     chosen = jnp.where((source == place + dp * out_lanes) & (place < out_lanes), 1.0, 0.0).astype(BF16)
     g_fc2[...] = dot_cols(matmul(gb_rows, chosen).astype(BF16), act_s[...])[0:out_lanes]
 
-    dense_attention(6, 12)
+    outs += [put_out(g_fc1, fc1_out), put_out(g_fc2, fc2_out)]
+    finish(vec_line)
+    vec_all[slot] = jnp.sum(vec_z[...], 0)
+    vec_last = to_plane(lambda peer: vec_all.at[slot], vec_all.at[slot], vec_all.at[0:others])
+
     dense_out()
-    dense_ff()
-
-    finish(vec_plane)
-    g_vec[...] = jnp.sum(vec_p[...], 0)
-    finish(ps_copies)
-    summed = jnp.sum(ps_recv[...].astype(F32), 0)
-    g_qkv[...] = summed[:, 0:576]
-    g_out[...] = summed[:, 640:832]
-    g_ip[...] = summed[:, 896:1024]
+    outs += [dense_ff(0), dense_ff(1)]
+
+    finish(pa_copies)
+    summed = jnp.sum(pa_recv[...].astype(F32), 0)
+    g_out[...] = summed[:, 0:192]
+    g_ip[...] = summed[:, 256:384]
     finish(pt_copies)
     g_tp[...] = jnp.sum(pt_recv[...].astype(F32), 0)
+    outs += [put_out(g_out, w_out_out), put_out(g_ip, ip_out), put_out(g_tp, tp_out)]
+    finish(vec_last)
+    g_vec[...] = vec_all[...].reshape(plane_size, 1152)
+    finish(ps_copies)
+    g_qkv[...] = jnp.sum(ps_recv[...].astype(F32), 0)
+    outs += [put_out(g_qkv, qkv_out)]
+    for copy in outs:
+        copy.wait()
     assert used[0] <= counter
+
+
+def finish_kernel(scale, *refs):
+    sources, vec, targets, outs, holds, sem = refs[0:9], refs[9], refs[10:19], refs[19:30], refs[30:39], refs[39]
+    pieces = []
+    for source, target, hold in zip(sources, targets, holds):
+        parts = 5 if source.shape[0] > 400 else 1
+        size = source.shape[0] // parts
+        for first in range(0, source.shape[0], size):
+            rows = pl.ds(first, size)
+            index = 2 * len(pieces)
+            pieces.append((
+                pltpu.make_async_copy(source.at[rows], hold.at[rows], sem.at[index]),
+                pltpu.make_async_copy(hold.at[rows], target.at[rows], sem.at[index + 1]),
+            ))
+    for fetch, _ in pieces:
+        fetch.start()
+    for fetch, store in pieces:
+        fetch.wait()
+        store.start()
+    fc1_bias, ln1_gain, ln1_bias, ln2_gain, ln2_bias, post_gain, post_bias, text_gain, text_bias, loss, log_scale = outs
+    for index, out in enumerate((ln1_gain, ln1_bias, ln2_gain, ln2_bias, post_gain, post_bias)):
+        out[...] = vec[index : index + 1, 0:WIDTH].reshape(WIDTH)
+    text_gain[...] = vec[6:7, 0:EMBED].reshape(EMBED)
+    text_bias[...] = vec[7:8, 0:EMBED].reshape(EMBED)
+    fc1_bias[...] = jnp.concatenate([vec[index : index + 1, WIDTH:] for index in range(8)], 1).reshape(HIDDEN)
+    loss[...] = (vec[6:7, EMBED : EMBED + 128] * scale).reshape(128)[0:1]
+    log_scale[...] = vec[7:8, EMBED : EMBED + 128].reshape(128)[0:1]
+    for _, store in pieces:
+        store.wait()
 
 
 def fused_shards(
@@ -877,7 +952,7 @@
     spread = HEADS * images_here
     line = planes * captions_here
     total_images = plane_size * planes * images_here
-    copies = 192
+    copies = 50
     vmem = pl.BlockSpec(memory_space=pltpu.VMEM)
     hbm = pl.BlockSpec(memory_space=pl.ANY)
 
@@ -900,30 +975,33 @@
         ((8, 1152), F32),
     )
     scratch = [
-        b16(WIDTH, 3 * WIDTH), b16(WIDTH, WIDTH), b16(WIDTH, HIDDEN), b16(HIDDEN, WIDTH),
+        b16(rows_all, WIDTH), b16(WIDTH, 3 * WIDTH), b16(WIDTH, WIDTH), b16(WIDTH, HIDDEN), b16(HIDDEN, WIDTH),
         b16(WIDTH, EMBED), b16(EMBED, EMBED),
         b16(rows_all, WIDTH), b16(rows_all, 2 * WIDTH), b16(rows_all, WIDTH), b16(rows_all, WIDTH),
-        f32(rows_all, WIDTH), b16(rows_all, WIDTH), f32(rows_all // 2, WIDTH), f32(rows_all, WIDTH),
+        f32(rows_all, WIDTH), b16(rows_all, WIDTH), b16(rows_all, WIDTH), f32(rows_all, WIDTH),
+        *(pltpu.VMEM(shape, kind) for shape, kind in out_shapes[2:9]),
         f32(spread, rows_all), b16(spread, rows_all), b16(2 * spread, rows_all), b16(2 * spread, WIDTH),
         f32(images_here, HIDDEN), f32(2, images_here, WIDTH),
         b16(planes, captions_here, EMBED), f32(planes, captions_here, 128),
         b16(plane_size, images_here, EMBED), f32(plane_size, images_here, 128),
         f32(plane_size, 8, plane_size * images_here), f32(planes, 8, line),
-        f32(plane_size, images_here, EMBED), f32(plane_size, images_here, EMBED),
-        f32(planes, captions_here, EMBED), f32(planes, captions_here, EMBED),
-        b16(planes, plane_size, images_here, WIDTH), b16(planes, plane_size, images_here, WIDTH),
-        b16(sides, 3 * HEADS, images_here, planes * block),
+        b16(plane_size, images_here, EMBED), b16(plane_size, images_here, EMBED),
+        b16(planes, captions_here, EMBED), b16(planes, captions_here, EMBED),
+        b16(planes, dp_size // 2, 2, sides, images_here, WIDTH), b16(planes, dp_size // 2, 2, sides, images_here, WIDTH),
+        b16(sides, 2 * HEADS, images_here, planes * block),
         b16(heads_here, plane_size, images_here, planes * block),
         b16(sides, 2, images_here, planes * block), b16(2, plane_size, images_here, planes * block),
+        b16(sides, images_here, planes * block), b16(plane_size, images_here, planes * block),
         b16(sides, captions_here, planes * text_block), b16(plane_size, captions_here, planes * text_block),
-        b16(dp_size, images_here, 1024), b16(plane_size, images_here, 1024),
+        b16(dp_size, images_here, 384), b16(plane_size, images_here, 384),
+        b16(dp_size, images_here, 640), b16(plane_size, images_here, 640),
         b16(dp_size, captions_here, 128), b16(plane_size, captions_here, 128),
-        b16(planes, block, 1024), b16(planes, block, 1024),
+        b16(planes, block, 384), b16(planes, block, 384), b16(planes, block, 576), b16(planes, block, 576),
         b16(planes, text_block, 128), b16(planes, text_block, 128),
-        f32(planes, 8, 1152), f32(plane_size, 8, 1152),
+        f32(8, 1, 1152), f32(plane_size, 1, 1152), f32(planes, 1, 1152), f32(plane_size, 1, 1152),
         f32(total_images, HIDDEN // dp_size), b16(total_images, HIDDEN // rep_size),
         b16(total_images, HIDDEN // dp_size), b16(total_images, 128),
-        pltpu.SemaphoreType.DMA((8,)), pltpu.SemaphoreType.DMA((copies,)), pltpu.SemaphoreType.DMA((copies,)),
+        pltpu.SemaphoreType.DMA((20,)), pltpu.SemaphoreType.DMA((copies,)), pltpu.SemaphoreType.DMA((copies,)),
     ]
     rows = images.transpose(1, 0, 2).reshape(rows_all, width)
     results = pl.pallas_call(
@@ -931,47 +1009,41 @@
             fused_kernel, (images_here, captions_here, planes, sides, dp_size), copies
         ),
         out_shape=tuple(jax.ShapeDtypeStruct(shape, kind) for shape, kind in out_shapes),
-        in_specs=[vmem] + [hbm] * 6 + [vmem] * 13,
-        out_specs=tuple(vmem for _ in out_shapes),
+        in_specs=[hbm] * 7 + [vmem] * 13,
+        out_specs=(hbm,) * 9 + (vmem,),
         scratch_shapes=scratch,
         compiler_params=pltpu.CompilerParams(
-            collective_id=1, has_side_effects=True, vmem_limit_bytes=60 * 2**20
+            collective_id=1, has_side_effects=True, vmem_limit_bytes=62 * 2**20
         ),
         name="fused_block",
     )(
         rows, qkv_weight, out_weight, fc1_weight, fc2_weight, image_proj, text_proj,
-        fc1_bias.reshape(1, -1), ln1_gain.reshape(1, -1), ln1_bias.reshape(1, -1),
-        ln2_gain.reshape(1, -1), ln2_bias.reshape(1, -1), post_gain.reshape(1, -1),
-        post_bias.reshape(1, -1), text_feats, text_gain.reshape(1, -1), text_bias.reshape(1, -1),
-        log_scale.reshape(1, 1), caption_counts.reshape(1, -1), positives.reshape(1, -1),
-    )
-    block_out, grad_images, g_qkv, g_out, g_fc1, g_fc2, g_ip, g_text, g_tp, g_vec = results
+        fc1_bias, ln1_gain, ln1_bias, ln2_gain, ln2_bias, post_gain, post_bias,
+        text_feats, text_gain, text_bias, log_scale, caption_counts, positives,
+    )
+    vectors = (HIDDEN,) + (WIDTH,) * 6 + (EMBED,) * 2 + (1, 1)
+    finals = pl.pallas_call(
+        functools.partial(finish_kernel, 1.0 / (images_here * dp_size * rep_size)),
+        out_shape=tuple(jax.ShapeDtypeStruct(shape, kind) for shape, kind in out_shapes[:9])
+        + tuple(jax.ShapeDtypeStruct((size,), F32) for size in vectors),
+        in_specs=[hbm] * 9 + [vmem],
+        out_specs=(hbm,) * 9 + (vmem,) * 11,
+        scratch_shapes=[pltpu.VMEM(shape, kind) for shape, kind in out_shapes[:9]]
+        + [pltpu.SemaphoreType.DMA((64,))],
+        compiler_params=pltpu.CompilerParams(vmem_limit_bytes=62 * 2**20),
+        name="results",
+    )(*results)
+    block_out, grad_images, g_qkv, g_out, g_fc1, g_fc2, g_ip, g_text, g_tp = finals[:9]
+    g_fc1_bias, ln1_gain, ln1_bias, ln2_gain, ln2_bias, post_gain, post_bias, text_gain, text_bias = finals[9:18]
+    loss, g_log_scale = finals[18:]
 
     def restore(values):
         return values.reshape(patches, images_here, width).transpose(1, 0, 2)
 
-    image_total = images_here * dp_size * rep_size
     return (
-        restore(block_out),
-        g_vec[6, EMBED] / image_total,
-        restore(grad_images),
-        g_qkv,
-        g_out,
-        g_fc1,
-        g_vec[:, WIDTH:].reshape(-1),
-        g_fc2.T,
-        g_vec[0, 0:WIDTH],
-        g_vec[1, 0:WIDTH],
-        g_vec[2, 0:WIDTH],
-        g_vec[3, 0:WIDTH],
-        g_vec[4, 0:WIDTH],
-        g_vec[5, 0:WIDTH],
-        g_ip,
-        g_text,
-        g_vec[6, 0:EMBED],
-        g_vec[7, 0:EMBED],
-        g_tp,
-        g_vec[7, EMBED : EMBED + 1],
+        restore(block_out), loss.reshape(()), restore(grad_images), g_qkv, g_out, g_fc1, g_fc1_bias, g_fc2.T,
+        ln1_gain, ln1_bias, ln2_gain, ln2_bias, post_gain, post_bias, g_ip, g_text, text_gain, text_bias,
+        g_tp, g_log_scale,
     )
 
 

time: 120 us -> 78 us (0.65)
  the two profiles are of different devices: /device:TPU:0 before, /device:TPU:4 now
where the time goes in v2:
time: 78 us; the launch traced here: 77.7 us
  Pallas kernels  76.2 us (98%)
  between operations  1.5 us (2%)
    pallas_call x1, Pallas kernels, fused_shards(): pl.pallas_call(functools.partial(fused_kernel, (images_here, captions_her...  69.9 us
    pallas_call x1, Pallas kernels, fused_shards(): pl.pallas_call(functools.partial(finish_kernel, 1.0 / (images_here * dp_s...  6.32 us

profile of v2, /device:TPU:4, one launch (start us, length us, event | category | flops | bytes accessed | tf_op | source)
XLA Modules:
  0.0 77.7 jit_solution(13954538564805108663)
XLA Ops:
  1.3 69.9 %fused_block.1 = (bf16[800,768]{1,0:T(8,128)(2,1)}, f32[800,768]{1,0:T(8,128)}, f32[96,576]{1,0:T(8,128)}, f32[96,192]{1,0:T(8,128)}, f32[96,768]{1,0:T(8,128)},...) custom-call(bf16[800,768]{1,0:T(8,128)(2,1)} %bitcast.11, ...), custom_call_target="tpu_custom_call" | custom-call | tf_op jit(solution)/shard_map/fused_block/pallas_call | solution.py:1007
  71.2 6.3 %results.1 = (bf16[800,768]{1,0:T(8,128)(2,1)}, f32[800,768]{1,0:T(8,128)}, f32[96,576]{1,0:T(8,128)}, f32[96,192]{1,0:T(8,128)}, f32[96,768]{1,0:T(8,128)}, /*i...) custom-call(bf16[800,768]{1,0:T(8,128)(2,1)} %get-tuple-element.50.r, ...), custom_call_target="tpu_custom_call" | custom-call | tf_op jit(solution)/shard_map/results/pallas_call | solution.py:1025

commit v3 on v2

--- a/solution.py
+++ b/solution.py
@@ -338,9 +338,10 @@
 
 def fused_kernel(dims, counter, *refs):
     (
-        x_hbm, qkv_hbm, out_hbm, fc1_hbm, fc2_hbm, ip_hbm, tp_hbm, fc1_bias_in,
-        ln1_gain_in, ln1_bias_in, ln2_gain_in, ln2_bias_in, post_gain_in, post_bias_in,
-        text_feats, text_gain_in, text_bias_in, log_scale_in, caption_counts, positives,
+        x_hbm, qkv_hbm, out_hbm, fc1_hbm, fc2_hbm, ip_hbm, tp_hbm
+    ) = refs[:7]
+    smalls = refs[7:20]
+    (
         block_hbm, images_hbm, qkv_out, w_out_out, fc1_out, fc2_out, ip_out, text_out, tp_out, g_vec,
         x, qkv, w_out, fc1, fc2, ip, tp,
         ni, kv, qd, mixed, middle, nmd, block_out, grad_images,
@@ -351,9 +352,13 @@
         gi_send, gi_recv, gt_send, gt_recv,
         nm_full, gb_full, rf_out, rf_in, ro_out, ro_in, cn_out, cn_in, tn_out, tn_in,
         ca_out, ca_in, co_out, co_in, te_out, te_in, pa_send, pa_recv, ps_send, ps_recv, pt_send, pt_recv,
-        vec_out, vec_in, vec_z, vec_all, hid_s, act_s, gh_s, nm_sel,
-        local_sem, send_sem, recv_sem,
-    ) = refs
+        vec_out, vec_in, vec_mid, vec_all, hid_s, act_s, gh_s, nm_sel,
+        local_sem, send_sem, recv_sem, *small_refs,
+    ) = refs[20:]
+    (
+        fc1_bias_in, ln1_gain_in, ln1_bias_in, ln2_gain_in, ln2_bias_in, post_gain_in, post_bias_in,
+        text_feats, text_gain_in, text_bias_in, log_scale_in, caption_counts, positives,
+    ) = small_refs
     images_here, captions_here, planes, sides, dp_size = dims
     plane_size = dp_size * sides
     rep_size = planes * sides
@@ -373,12 +378,7 @@
     text_ratio = image_total / caption_total
 
     used = [0]
-    fc1_bias = fc1_bias_in[...].reshape(1, HIDDEN)
-    ln1_gain, ln1_bias, ln2_gain, ln2_bias, post_gain, post_bias = (
-        ref[...].reshape(1, WIDTH)
-        for ref in (ln1_gain_in, ln1_bias_in, ln2_gain_in, ln2_bias_in, post_gain_in, post_bias_in)
-    )
-    text_gain, text_bias = (ref[...].reshape(1, EMBED) for ref in (text_gain_in, text_bias_in))
+    unsent = []
 
     def plane_peer(step):
         peer = lax.rem(slot + step, plane_size)
@@ -426,11 +426,15 @@
     def finish(sent):
         whole, index = sent
         pltpu.make_async_copy(whole, whole, recv_sem.at[index]).wait()
-        pltpu.make_async_copy(whole, whole, send_sem.at[index]).wait()
+        unsent.append(pltpu.make_async_copy(whole, whole, send_sem.at[index]))
 
     others = plane_size - 1
     lines = planes - 1
 
+    small_loads = []
+    for index, (source, target) in enumerate(zip(smalls, small_refs)):
+        small_loads.append(pltpu.make_async_copy(source, target, local_sem.at[20 + index]))
+        small_loads[-1].start()
     loads = []
 
     def put_out(source, target):
@@ -454,6 +458,15 @@
         pl.semaphore_signal(barrier, inc=1, device_id=plane_peer(step)[1], device_id_type=MESH)
     for step in range(1, planes):
         pl.semaphore_signal(barrier, inc=1, device_id=line_peer(step)[1], device_id_type=MESH)
+
+    for load in small_loads:
+        load.wait()
+    fc1_bias = fc1_bias_in[...].reshape(1, HIDDEN)
+    ln1_gain, ln1_bias, ln2_gain, ln2_bias, post_gain, post_bias = (
+        ref[...].reshape(1, WIDTH)
+        for ref in (ln1_gain_in, ln1_bias_in, ln2_gain_in, ln2_bias_in, post_gain_in, post_bias_in)
+    )
+    text_gain, text_bias = (ref[...].reshape(1, EMBED) for ref in (text_gain_in, text_bias_in))
 
     text_full, _, _ = layer_norm(text_feats[...].astype(F32), text_gain, text_bias)
     text_norm = text_full.astype(BF16)
@@ -549,7 +562,7 @@
                 rf_out.at[lax.rem(peer, sides), pl.ds(lax.rem(first + HEADS, 2 * HEADS), bundle)],
                 rf_in.at[pl.ds(part * bundle, bundle), slot], device, take(), arrivals + part,
             )
-            rf_copies.append((copy, first))
+            rf_copies.append((copy, first, part))
 
     def head_kind(first):
         return first // HEADS
@@ -602,6 +615,7 @@
         return put_out(block_out.at[rows], block_hbm.at[rows])
 
     dense_query()
+    dense_attention(0, 2)
 
     finish(text_copies)
     finish(pos_copies)
@@ -628,7 +642,10 @@
     row_copies = to_plane(lambda peer: row_sum.at[slot], row_sum.at[slot], row_sum.at[0:others])
     col_copies = to_line(lambda peer: col_sum.at[z], col_sum.at[z], col_sum.at[0:lines])
 
-    dense_attention(0, 6)
+    for copy, first, part in rf_copies:
+        if part < 2:
+            pl.when(head_kind(first) == 2)(copy.start)
+    dense_attention(2, 8)
 
     finish(row_copies)
     finish(col_copies)
@@ -655,12 +672,14 @@
     gt_copies = to_line(lambda peer: gt_send.at[peer], gt_recv.at[z], gt_recv.at[0:lines])
     gt_recv[z] = gt_send[z]
 
-    dense_attention(6, 12)
+    dense_attention(8, 12)
+    dense_out()
 
     finish(gi_copies)
     cn_copies = to_plane(lambda peer: cn_out.at[lax.rem(peer, sides)], cn_in.at[slot], cn_in.at[0:others])
-    for copy, first in rf_copies:
-        pl.when(head_kind(first) == 2)(copy.start)
+    for copy, first, part in rf_copies:
+        if part == 2:
+            pl.when(head_kind(first) == 2)(copy.start)
     grad_embed = unit_back(jnp.sum(gi_recv[...].astype(F32), 0), image_unit, image_factor).astype(BF16)
     grad_class, g_post_gain, g_post_bias = norm_back(
         dot_rows(grad_embed, ip[...]), small[1], factor_post, post_gain
@@ -716,7 +735,7 @@
     co_out[2, :, 384:576] = grad_v[:, 0:192].astype(BF16)
     co_out[3, :, 0:576] = v_shift[:, 128:704].astype(BF16)
     co_copies = to_plane(lambda peer: co_out.at[peer // sides], co_in.at[slot], co_in.at[0:others])
-    for copy, first in rf_copies:
+    for copy, first, _ in rf_copies:
         pl.when(head_kind(first) == 1)(copy.start)
     co_in[slot] = co_out[dp]
     for part in range(3):
@@ -727,18 +746,6 @@
             rf_in[part * bundle : (part + 1) * bundle, slot] = own
 
         pl.when(head_kind(mine) > 0)(keep)
-
-    rows_here = planes * block_lanes
-    finish(ro_copies)
-    finish(cn_copies)
-    finish(ca_copies)
-    columns_in = ca_in[...].reshape(plane_images, 384)
-    got = dot_cols(ro_in[0].reshape(plane_images, rows_here), columns_in[:, 0:256])
-    pa_send[:, :, 0:256] = got.astype(BF16).reshape(planes, block_lanes, 256)
-    got = dot_cols(cn_in[...].reshape(plane_images, rows_here), columns_in[:, 256:384])
-    pa_send[:, :, 256:384] = got.astype(BF16).reshape(planes, block_lanes, 128)
-    pa_copies = to_line(lambda peer: pa_send.at[peer], pa_recv.at[z], pa_recv.at[0:lines])
-    pa_recv[z] = pa_send[z]
 
     finish(gt_copies)
     grad_text = unit_back(jnp.sum(gt_recv[...].astype(F32), 0), text_unit, text_factor).astype(BF16)
@@ -752,10 +759,9 @@
     )
     g_text[...] = g_feats
 
+
     finish(nm_line)
     nm_chips = to_chips(nm_full)
-    finish(gb_line)
-    gb_chips = to_chips(gb_full)
 
     uu[0 : HEADS * images_here] = dot_rows(query_spread, qkv[:, WIDTH : 2 * WIDTH]).astype(BF16)
     uu[HEADS * images_here :] = dot_rows(mixed_spread, qkv[:, 2 * WIDTH :]).astype(BF16)
@@ -782,13 +788,26 @@
         g_text_gain[None], g_text_bias[None],
     )
     for index, vector in enumerate(vectors):
-        vec_out[index, :, 0 : vector.shape[1]] = vector
-        vec_out[index, :, WIDTH:] = g_fc1_bias[:, index * 384 : index * 384 + 384]
+        row = slice(index % 2, index % 2 + 1)
+        vec_out[index // 2, row, 0 : vector.shape[1]] = vector
+        vec_out[index // 2, row, WIDTH:] = g_fc1_bias[:, index * 384 : index * 384 + 384]
     first_lane = lax.broadcasted_iota(jnp.int32, (1, 256), 1) == 0
-    vec_out[6, :, EMBED:WIDTH] = jnp.where(first_lane, loss_part, 0.0)
-    vec_out[7, :, EMBED:WIDTH] = jnp.where(first_lane, scale_part, 0.0)
-    vec_plane = to_plane(lambda peer: vec_out.at[peer], vec_in.at[slot], vec_in.at[0:others])
-    vec_in[slot] = vec_out[slot]
+    vec_out[3, 0:1, EMBED:WIDTH] = jnp.where(first_lane, loss_part, 0.0)
+    vec_out[3, 1:2, EMBED:WIDTH] = jnp.where(first_lane, scale_part, 0.0)
+    vec_line = to_line(lambda peer: vec_out.at[peer], vec_in.at[z], vec_in.at[0:lines])
+    vec_in[z] = vec_out[z]
+
+    rows_here = planes * block_lanes
+    finish(ro_copies)
+    finish(cn_copies)
+    finish(ca_copies)
+    columns_in = ca_in[...].reshape(plane_images, 384)
+    got = dot_cols(ro_in[0].reshape(plane_images, rows_here), columns_in[:, 0:256])
+    pa_send[:, :, 0:256] = got.astype(BF16).reshape(planes, block_lanes, 256)
+    got = dot_cols(cn_in[...].reshape(plane_images, rows_here), columns_in[:, 256:384])
+    pa_send[:, :, 256:384] = got.astype(BF16).reshape(planes, block_lanes, 128)
+    pa_copies = to_line(lambda peer: pa_send.at[peer], pa_recv.at[z], pa_recv.at[0:lines])
+    pa_recv[z] = pa_send[z]
 
     for part in range(3):
         mine = dp * heads_here + part * bundle
@@ -816,8 +835,6 @@
         )
     ps_copies = to_line(lambda peer: ps_send.at[peer], ps_recv.at[z], ps_recv.at[0:lines])
     ps_recv[z] = ps_send[z]
-    for copy, first in rf_copies:
-        pl.when(head_kind(first) > 0)(copy.wait_send)
     finish(tn_copies)
     finish(te_copies)
     got = dot_cols(
@@ -828,14 +845,22 @@
     pt_copies = to_line(lambda peer: pt_send.at[peer], pt_recv.at[z], pt_recv.at[0:lines])
     pt_recv[z] = pt_send[z]
 
+    finish(vec_line)
+    vec_mid[slot] = jnp.sum(vec_in[...], 0)
+    vec_plane = to_plane(lambda peer: vec_mid.at[slot], vec_mid.at[slot], vec_mid.at[0:others])
+    finish(gb_line)
+    gb_chips = to_chips(gb_full)
+
+    outs += [dense_ff(0)]
     finish(vec_plane)
-    vec_z[z] = jnp.sum(vec_in[...], 0)
-    vec_line = to_line(lambda peer: vec_z.at[z], vec_z.at[z], vec_z.at[0:lines])
+    vec_all[z] = jnp.sum(vec_mid[...], 0)
+    vec_last = to_line(lambda peer: vec_all.at[z], vec_all.at[z], vec_all.at[0:lines])
     finish(nm_chips)
     nm_partner = to_partner(nm_full)
-
     finish(gb_chips)
     gb_partner = to_partner(gb_full)
+    outs += [dense_ff(1)]
+
     finish(nm_partner)
     all_rows = plane_images * planes
     nm_rows = nm_full[...].reshape(all_rows, WIDTH)
@@ -848,6 +873,7 @@
     place = lax.broadcasted_iota(jnp.int32, (WIDTH, 128), 1)
     chosen = jnp.where((source == place + rep * block_lanes) & (place < block_lanes), 1.0, 0.0).astype(BF16)
     nm_sel[...] = matmul(nm_rows, chosen).astype(BF16)
+
     finish(gb_partner)
     gb_rows = gb_full[...].reshape(all_rows, WIDTH)
     gate = jax.nn.sigmoid(1.702 * hid_s[...])
@@ -862,12 +888,6 @@
     g_fc2[...] = dot_cols(matmul(gb_rows, chosen).astype(BF16), act_s[...])[0:out_lanes]
 
     outs += [put_out(g_fc1, fc1_out), put_out(g_fc2, fc2_out)]
-    finish(vec_line)
-    vec_all[slot] = jnp.sum(vec_z[...], 0)
-    vec_last = to_plane(lambda peer: vec_all.at[slot], vec_all.at[slot], vec_all.at[0:others])
-
-    dense_out()
-    outs += [dense_ff(0), dense_ff(1)]
 
     finish(pa_copies)
     summed = jnp.sum(pa_recv[...].astype(F32), 0)
@@ -877,34 +897,39 @@
     g_tp[...] = jnp.sum(pt_recv[...].astype(F32), 0)
     outs += [put_out(g_out, w_out_out), put_out(g_ip, ip_out), put_out(g_tp, tp_out)]
     finish(vec_last)
-    g_vec[...] = vec_all[...].reshape(plane_size, 1152)
+    g_vec[...] = vec_all[...].reshape(8, 1152)
     finish(ps_copies)
     g_qkv[...] = jnp.sum(ps_recv[...].astype(F32), 0)
     outs += [put_out(g_qkv, qkv_out)]
-    for copy in outs:
+    for copy in outs + unsent:
         copy.wait()
+    for copy, first, _ in rf_copies:
+        pl.when(head_kind(first) > 0)(copy.wait_send)
     assert used[0] <= counter
 
 
 def finish_kernel(scale, *refs):
-    sources, vec, targets, outs, holds, sem = refs[0:9], refs[9], refs[10:19], refs[19:30], refs[30:39], refs[39]
+    sources, vec_hbm, targets, outs_hbm = refs[0:9], refs[9], refs[10:19], refs[19:30]
+    holds, vec, outs, sem = refs[30:39], refs[39], refs[40:51], refs[51]
+    count = 0
+
+    def copy(source, target):
+        nonlocal count
+        count += 1
+        return pltpu.make_async_copy(source, target, sem.at[count - 1])
+
+    vec_load = copy(vec_hbm, vec)
+    vec_load.start()
     pieces = []
     for source, target, hold in zip(sources, targets, holds):
         parts = 5 if source.shape[0] > 400 else 1
         size = source.shape[0] // parts
         for first in range(0, source.shape[0], size):
             rows = pl.ds(first, size)
-            index = 2 * len(pieces)
-            pieces.append((
-                pltpu.make_async_copy(source.at[rows], hold.at[rows], sem.at[index]),
-                pltpu.make_async_copy(hold.at[rows], target.at[rows], sem.at[index + 1]),
-            ))
-    for fetch, _ in pieces:
-        fetch.start()
-    for fetch, store in pieces:
-        fetch.wait()
-        store.start()
+            pieces.append((copy(source.at[rows], hold.at[rows]), copy(hold.at[rows], target.at[rows])))
+            pieces[-1][0].start()
     fc1_bias, ln1_gain, ln1_bias, ln2_gain, ln2_bias, post_gain, post_bias, text_gain, text_bias, loss, log_scale = outs
+    vec_load.wait()
     for index, out in enumerate((ln1_gain, ln1_bias, ln2_gain, ln2_bias, post_gain, post_bias)):
         out[...] = vec[index : index + 1, 0:WIDTH].reshape(WIDTH)
     text_gain[...] = vec[6:7, 0:EMBED].reshape(EMBED)
@@ -912,7 +937,15 @@
     fc1_bias[...] = jnp.concatenate([vec[index : index + 1, WIDTH:] for index in range(8)], 1).reshape(HIDDEN)
     loss[...] = (vec[6:7, EMBED : EMBED + 128] * scale).reshape(128)[0:1]
     log_scale[...] = vec[7:8, EMBED : EMBED + 128].reshape(128)[0:1]
-    for _, store in pieces:
+    stores = []
+    for out, target in zip(outs, outs_hbm):
+        stores.append(copy(out, target))
+        stores[-1].start()
+    for fetch, store in pieces:
+        fetch.wait()
+        store.start()
+        stores.append(store)
+    for store in stores:
         store.wait()
 
 
@@ -974,6 +1007,10 @@
         ((text_block, EMBED // dp_size), F32),
         ((8, 1152), F32),
     )
+    vectors = (
+        fc1_bias, ln1_gain, ln1_bias, ln2_gain, ln2_bias, post_gain, post_bias,
+        text_feats, text_gain, text_bias, log_scale, caption_counts, positives,
+    )
     scratch = [
         b16(rows_all, WIDTH), b16(WIDTH, 3 * WIDTH), b16(WIDTH, WIDTH), b16(WIDTH, HIDDEN), b16(HIDDEN, WIDTH),
         b16(WIDTH, EMBED), b16(EMBED, EMBED),
@@ -998,10 +1035,11 @@
         b16(dp_size, captions_here, 128), b16(plane_size, captions_here, 128),
         b16(planes, block, 384), b16(planes, block, 384), b16(planes, block, 576), b16(planes, block, 576),
         b16(planes, text_block, 128), b16(planes, text_block, 128),
-        f32(8, 1, 1152), f32(plane_size, 1, 1152), f32(planes, 1, 1152), f32(plane_size, 1, 1152),
+        f32(4, 2, 1152), f32(planes, 2, 1152), f32(plane_size, 2, 1152), f32(planes, 2, 1152),
         f32(total_images, HIDDEN // dp_size), b16(total_images, HIDDEN // rep_size),
         b16(total_images, HIDDEN // dp_size), b16(total_images, 128),
-        pltpu.SemaphoreType.DMA((20,)), pltpu.SemaphoreType.DMA((copies,)), pltpu.SemaphoreType.DMA((copies,)),
+        pltpu.SemaphoreType.DMA((33,)), pltpu.SemaphoreType.DMA((copies,)), pltpu.SemaphoreType.DMA((copies,)),
+        *(pltpu.VMEM(value.shape, value.dtype) for value in vectors),
     ]
     rows = images.transpose(1, 0, 2).reshape(rows_all, width)
     results = pl.pallas_call(
@@ -1009,7 +1047,7 @@
             fused_kernel, (images_here, captions_here, planes, sides, dp_size), copies
         ),
         out_shape=tuple(jax.ShapeDtypeStruct(shape, kind) for shape, kind in out_shapes),
-        in_specs=[hbm] * 7 + [vmem] * 13,
+        in_specs=[hbm] * 20,
         out_specs=(hbm,) * 9 + (vmem,),
         scratch_shapes=scratch,
         compiler_params=pltpu.CompilerParams(
@@ -1018,18 +1056,18 @@
         name="fused_block",
     )(
         rows, qkv_weight, out_weight, fc1_weight, fc2_weight, image_proj, text_proj,
-        fc1_bias, ln1_gain, ln1_bias, ln2_gain, ln2_bias, post_gain, post_bias,
-        text_feats, text_gain, text_bias, log_scale, caption_counts, positives,
-    )
-    vectors = (HIDDEN,) + (WIDTH,) * 6 + (EMBED,) * 2 + (1, 1)
+        *vectors,
+    )
+    sizes = (HIDDEN,) + (WIDTH,) * 6 + (EMBED,) * 2 + (1, 1)
     finals = pl.pallas_call(
         functools.partial(finish_kernel, 1.0 / (images_here * dp_size * rep_size)),
         out_shape=tuple(jax.ShapeDtypeStruct(shape, kind) for shape, kind in out_shapes[:9])
-        + tuple(jax.ShapeDtypeStruct((size,), F32) for size in vectors),
-        in_specs=[hbm] * 9 + [vmem],
-        out_specs=(hbm,) * 9 + (vmem,) * 11,
-        scratch_shapes=[pltpu.VMEM(shape, kind) for shape, kind in out_shapes[:9]]
-        + [pltpu.SemaphoreType.DMA((64,))],
+        + tuple(jax.ShapeDtypeStruct((size,), F32) for size in sizes),
+        in_specs=[hbm] * 10,
+        out_specs=(hbm,) * 20,
+        scratch_shapes=[pltpu.VMEM(shape, kind) for shape, kind in out_shapes]
+        + [pltpu.VMEM((size,), F32) for size in sizes]
+        + [pltpu.SemaphoreType.DMA((46,))],
         compiler_params=pltpu.CompilerParams(vmem_limit_bytes=62 * 2**20),
         name="results",
     )(*results)

time: 78 us -> 66.5 us (0.85)
  the two profiles are of different devices: /device:TPU:4 before, /device:TPU:0 now
where the time goes in v3:
time: 66.5 us; the launch traced here: 66.3 us
  Pallas kernels  64.8 us (97%)
  between operations  1.5 us (2%)
    pallas_call x1, Pallas kernels, fused_shards(): pl.pallas_call(functools.partial(fused_kernel, (images_here, captions_her...  60.1 us
    pallas_call x1, Pallas kernels, fused_shards(): pl.pallas_call(functools.partial(finish_kernel, 1.0 / (images_here * dp_s...  4.74 us

profile of v3, /device:TPU:0, one launch (start us, length us, event | category | flops | bytes accessed | tf_op | source)
XLA Modules:
  0.0 66.3 jit_solution(928247264602591046)
XLA Ops:
  1.3 60.1 %fused_block.1 = (bf16[800,768]{1,0:T(8,128)(2,1)}, f32[800,768]{1,0:T(8,128)}, f32[96,576]{1,0:T(8,128)}, f32[96,192]{1,0:T(8,128)}, f32[96,768]{1,0:T(8,128)},...) custom-call(bf16[800,768]{1,0:T(8,128)(2,1)} %bitcast.11, ...), custom_call_target="tpu_custom_call" | custom-call | tf_op jit(solution)/shard_map/fused_block/pallas_call | solution.py:1045
  61.4 4.7 %results.1 = (bf16[800,768]{1,0:T(8,128)(2,1)}, f32[800,768]{1,0:T(8,128)}, f32[96,576]{1,0:T(8,128)}, f32[96,192]{1,0:T(8,128)}, f32[96,768]{1,0:T(8,128)}, /*i...) custom-call(bf16[800,768]{1,0:T(8,128)(2,1)} %get-tuple-element.50.r, ...), custom_call_target="tpu_custom_call" | custom-call | tf_op jit(solution)/shard_map/results/pallas_call | solution.py:1062

commit v4 on v3

--- a/solution.py
+++ b/solution.py
@@ -371,6 +371,7 @@
     slot = dp * sides + side
     row_y = dp // 2
     core = lax.rem(dp, 2)
+    chip = row_y * sides + side
     plane_images = plane_size * images_here
     line_captions = planes * captions_here
     image_total = plane_images * planes
@@ -413,14 +414,14 @@
     def to_chips(buffer):
         peers = []
         for step in range(1, 2 * sides):
-            peer = lax.rem(row_y * sides + side + step, 2 * sides)
+            peer = lax.rem(chip + step, 2 * sides)
             peers.append((peer, ((peer // sides) * 2 + core, z * sides + lax.rem(peer, sides))))
-        mine = buffer.at[:, row_y, core, side]
-        return exchange(peers, lambda peer: mine, mine, buffer.at[0 : planes - 1, 0])
+        mine = buffer.at[core, chip]
+        return exchange(peers, lambda peer: mine, mine, buffer.at[0, 0 : 2 * sides - 1])
 
     def to_partner(buffer):
         device = (row_y * 2 + 1 - core, rep)
-        mine = buffer.at[:, :, core]
+        mine = buffer.at[core]
         return exchange([(0, device)], lambda peer: mine, mine, mine)
 
     def finish(sent):
@@ -477,6 +478,18 @@
     pos_all[z] = jnp.transpose(pos_rows)
     cnt_rows = jnp.broadcast_to(caption_counts[...].reshape(1, images_here).astype(F32), (128, images_here))
     cnt_all[slot] = jnp.transpose(cnt_rows)
+    loads[1].wait()
+    for first in range(0, rows_all, STEP):
+        full = layer_norm(x[first : first + STEP, :].astype(F32), ln1_gain, ln1_bias)[0]
+        full = full.reshape(STEP // 16, 2, GROUP, WIDTH)
+        for part in range(2):
+            to = part * half + first // 2
+            ni[to : to + STEP // 2, :] = full[:, part].reshape(STEP // 2, WIDTH).astype(BF16)
+
+    loads[2].wait()
+    for first in range(0, 2 * WIDTH, WIDTH):
+        kv[:, first : first + WIDTH] = matmul(ni[...], qkv[:, WIDTH + first : 2 * WIDTH + first]).astype(BF16)
+
     pl.semaphore_wait(barrier, plane_size - 1 + planes - 1)
     text_copies = to_line(lambda peer: t_all.at[z], t_all.at[z], t_all.at[0:lines])
     pos_copies = to_line(lambda peer: pos_all.at[z], pos_all.at[z], pos_all.at[0:lines])
@@ -486,18 +499,6 @@
         tn_out[to_side] = pick_blocks(text_full, to_side, sides, text_lanes, planes).astype(BF16)
     tn_copies = to_plane(lambda peer: tn_out.at[lax.rem(peer, sides)], tn_in.at[slot], tn_in.at[0:others])
     tn_in[slot] = tn_out[side]
-
-    loads[1].wait()
-    for first in range(0, rows_all, STEP):
-        full = layer_norm(x[first : first + STEP, :].astype(F32), ln1_gain, ln1_bias)[0]
-        full = full.reshape(STEP // 16, 2, GROUP, WIDTH)
-        for part in range(2):
-            to = part * half + first // 2
-            ni[to : to + STEP // 2, :] = full[:, part].reshape(STEP // 2, WIDTH).astype(BF16)
-
-    loads[2].wait()
-    for first in range(0, 2 * WIDTH, WIDTH):
-        kv[:, first : first + WIDTH] = matmul(ni[...], qkv[:, WIDTH + first : 2 * WIDTH + first]).astype(BF16)
 
     resid_c = x[0:images_here, :].astype(F32)
     normed_c = layer_norm(resid_c, ln1_gain, ln1_bias)[0].astype(BF16)
@@ -519,15 +520,15 @@
         ro_out[to_side, 0] = pick_blocks(mixed_f, to_side, sides, block_lanes, planes).astype(BF16)
         ro_out[to_side, 1] = pick_blocks(normed_f, to_side, sides, block_lanes, planes).astype(BF16)
     ro_copies = to_plane(
-        lambda peer: ro_out.at[lax.rem(peer, sides)], ro_in.at[:, slot], ro_in.at[:, 0:others]
-    )
-    ro_in[:, slot] = ro_out[side]
+        lambda peer: ro_out.at[lax.rem(peer, sides)], ro_in.at[slot], ro_in.at[0:others]
+    )
+    ro_in[slot] = ro_out[side]
     loads[3].wait()
     middle_c = resid_c + matmul(mixed_c.astype(BF16), w_out[...])
     full, unit_two, factor_two = layer_norm(middle_c, ln2_gain, ln2_bias)
-    nm_full[z, row_y, core, side] = full.astype(BF16)
+    nm_full[core, chip, z] = full.astype(BF16)
     nm_line = to_line(
-        lambda peer: nm_full.at[z, row_y, core, side], nm_full.at[z, row_y, core, side], nm_full.at[0:lines, 0, 0, 0]
+        lambda peer: nm_full.at[core, chip, z], nm_full.at[core, chip, z], nm_full.at[0, 0, 0:lines]
     )
     loads[4].wait()
     hid_c[...] = matmul(full.astype(BF16), fc1[...]) + fc1_bias
@@ -560,7 +561,7 @@
             first = (peer // sides) * heads_here + part * bundle
             copy = copy_to(
                 rf_out.at[lax.rem(peer, sides), pl.ds(lax.rem(first + HEADS, 2 * HEADS), bundle)],
-                rf_in.at[pl.ds(part * bundle, bundle), slot], device, take(), arrivals + part,
+                rf_in.at[slot, pl.ds(part * bundle, bundle)], device, 32 + len(rf_copies), arrivals + part,
             )
             rf_copies.append((copy, first, part))
 
@@ -615,6 +616,7 @@
         return put_out(block_out.at[rows], block_hbm.at[rows])
 
     dense_query()
+    uu[0 : HEADS * images_here] = dot_rows(query_spread, qkv[:, WIDTH : 2 * WIDTH]).astype(BF16)
     dense_attention(0, 2)
 
     finish(text_copies)
@@ -685,9 +687,9 @@
         dot_rows(grad_embed, ip[...]), small[1], factor_post, post_gain
     )
     gb_low = grad_class.astype(BF16)
-    gb_full[z, row_y, core, side] = gb_low
+    gb_full[core, chip, z] = gb_low
     gb_line = to_line(
-        lambda peer: gb_full.at[z, row_y, core, side], gb_full.at[z, row_y, core, side], gb_full.at[0:lines, 0, 0, 0]
+        lambda peer: gb_full.at[core, chip, z], gb_full.at[core, chip, z], gb_full.at[0, 0, 0:lines]
     )
     gate = jax.nn.sigmoid(1.702 * hid_c[...])
     grad_hidden = (
@@ -716,11 +718,14 @@
     gsp[0 : HEADS * images_here] = grad_scores.astype(BF16)
     gsp[HEADS * images_here :] = attn_low[...]
     score_low = gsp[0 : HEADS * images_here]
-    grad_query = head_gather(matmul(score_low, kv[:, 0:WIDTH])).astype(BF16)
     key_rows = matmul(score_low, ni[...])
     for to_side in range(sides):
         picked = pick_blocks(key_rows, to_side, sides, block_lanes, planes).astype(BF16)
         rf_out[to_side, 0:HEADS] = picked.reshape(HEADS, images_here, planes * block_lanes)
+
+    for copy, first, _ in rf_copies:
+        pl.when(head_kind(first) == 1)(copy.start)
+    grad_query = head_gather(matmul(score_low, kv[:, 0:WIDTH])).astype(BF16)
 
     grad_q = grad_query.astype(F32)
     query_f = query_c.astype(F32)
@@ -735,15 +740,13 @@
     co_out[2, :, 384:576] = grad_v[:, 0:192].astype(BF16)
     co_out[3, :, 0:576] = v_shift[:, 128:704].astype(BF16)
     co_copies = to_plane(lambda peer: co_out.at[peer // sides], co_in.at[slot], co_in.at[0:others])
-    for copy, first, _ in rf_copies:
-        pl.when(head_kind(first) == 1)(copy.start)
     co_in[slot] = co_out[dp]
     for part in range(3):
         mine = dp * heads_here + part * bundle
 
         def keep(part=part, mine=mine):
             own = rf_out[side, pl.ds(lax.rem(mine + HEADS, 2 * HEADS), bundle)]
-            rf_in[part * bundle : (part + 1) * bundle, slot] = own
+            rf_in[slot, part * bundle : (part + 1) * bundle] = own
 
         pl.when(head_kind(mine) > 0)(keep)
 
@@ -763,7 +766,6 @@
     finish(nm_line)
     nm_chips = to_chips(nm_full)
 
-    uu[0 : HEADS * images_here] = dot_rows(query_spread, qkv[:, WIDTH : 2 * WIDTH]).astype(BF16)
     uu[HEADS * images_here :] = dot_rows(mixed_spread, qkv[:, 2 * WIDTH :]).astype(BF16)
     class_in = dot_rows(grad_query, qkv[:, 0:WIDTH])
 
@@ -802,7 +804,7 @@
     finish(cn_copies)
     finish(ca_copies)
     columns_in = ca_in[...].reshape(plane_images, 384)
-    got = dot_cols(ro_in[0].reshape(plane_images, rows_here), columns_in[:, 0:256])
+    got = dot_cols(ro_in[:, 0].reshape(plane_images, rows_here), columns_in[:, 0:256])
     pa_send[:, :, 0:256] = got.astype(BF16).reshape(planes, block_lanes, 256)
     got = dot_cols(cn_in[...].reshape(plane_images, rows_here), columns_in[:, 256:384])
     pa_send[:, :, 256:384] = got.astype(BF16).reshape(planes, block_lanes, 128)
@@ -811,12 +813,12 @@
 
     for part in range(3):
         mine = dp * heads_here + part * bundle
-        here = rf_in.at[part * bundle : (part + 1) * bundle, 0:others]
+        here = rf_in.at[0:others, part * bundle : (part + 1) * bundle]
         pl.when(head_kind(mine) > 0)(pltpu.make_async_copy(here, here, recv_sem.at[arrivals + part]).wait)
 
         def repeat(part=part):
-            rf_in[part * bundle : (part + 1) * bundle] = jnp.broadcast_to(
-                ro_in[1][None], (bundle, plane_size, images_here, rows_here)
+            rf_in[:, part * bundle : (part + 1) * bundle] = jnp.broadcast_to(
+                ro_in[:, 1][:, None], (plane_size, bundle, images_here, rows_here)
             )
 
         pl.when(head_kind(mine) == 0)(repeat)
@@ -825,9 +827,9 @@
     lane = lax.broadcasted_iota(jnp.int32, (rows_here, 128), 1)
     for tile in range(5):
         right = columns_in[:, tile * 128 : tile * 128 + 128]
-        got = dot_cols(rf_in[2 * tile].reshape(plane_images, rows_here), right)
+        got = dot_cols(rf_in[:, 2 * tile].reshape(plane_images, rows_here), right)
         if 2 * tile + 1 < heads_here:
-            other = dot_cols(rf_in[2 * tile + 1].reshape(plane_images, rows_here), right)
+            other = dot_cols(rf_in[:, 2 * tile + 1].reshape(plane_images, rows_here), right)
             got = jnp.where(lane < HDIM, got, other)
         width = min(128, 576 - tile * 128)
         ps_send[:, :, tile * 128 : tile * 128 + width] = (
@@ -922,7 +924,7 @@
     vec_load.start()
     pieces = []
     for source, target, hold in zip(sources, targets, holds):
-        parts = 5 if source.shape[0] > 400 else 1
+        parts = 2 if source.shape[0] > 400 else 1
         size = source.shape[0] // parts
         for first in range(0, source.shape[0], size):
             rows = pl.ds(first, size)
@@ -985,7 +987,7 @@
     spread = HEADS * images_here
     line = planes * captions_here
     total_images = plane_size * planes * images_here
-    copies = 50
+    copies = 32
     vmem = pl.BlockSpec(memory_space=pltpu.VMEM)
     hbm = pl.BlockSpec(memory_space=pl.ANY)
 
@@ -1024,10 +1026,10 @@
         f32(plane_size, 8, plane_size * images_here), f32(planes, 8, line),
         b16(plane_size, images_here, EMBED), b16(plane_size, images_here, EMBED),
         b16(planes, captions_here, EMBED), b16(planes, captions_here, EMBED),
-        b16(planes, dp_size // 2, 2, sides, images_here, WIDTH), b16(planes, dp_size // 2, 2, sides, images_here, WIDTH),
+        b16(2, dp_size // 2 * sides, planes, images_here, WIDTH), b16(2, dp_size // 2 * sides, planes, images_here, WIDTH),
         b16(sides, 2 * HEADS, images_here, planes * block),
-        b16(heads_here, plane_size, images_here, planes * block),
-        b16(sides, 2, images_here, planes * block), b16(2, plane_size, images_here, planes * block),
+        b16(plane_size, heads_here, images_here, planes * block),
+        b16(sides, 2, images_here, planes * block), b16(plane_size, 2, images_here, planes * block),
         b16(sides, images_here, planes * block), b16(plane_size, images_here, planes * block),
         b16(sides, captions_here, planes * text_block), b16(plane_size, captions_here, planes * text_block),
         b16(dp_size, images_here, 384), b16(plane_size, images_here, 384),
@@ -1038,7 +1040,7 @@
         f32(4, 2, 1152), f32(planes, 2, 1152), f32(plane_size, 2, 1152), f32(planes, 2, 1152),
         f32(total_images, HIDDEN // dp_size), b16(total_images, HIDDEN // rep_size),
         b16(total_images, HIDDEN // dp_size), b16(total_images, 128),
-        pltpu.SemaphoreType.DMA((33,)), pltpu.SemaphoreType.DMA((copies,)), pltpu.SemaphoreType.DMA((copies,)),
+        pltpu.SemaphoreType.DMA((33,)), pltpu.SemaphoreType.DMA((32 + 3 * (plane_size - 1),)), pltpu.SemaphoreType.DMA((copies,)),
         *(pltpu.VMEM(value.shape, value.dtype) for value in vectors),
     ]
     rows = images.transpose(1, 0, 2).reshape(rows_all, width)
@@ -1067,7 +1069,7 @@
         out_specs=(hbm,) * 20,
         scratch_shapes=[pltpu.VMEM(shape, kind) for shape, kind in out_shapes]
         + [pltpu.VMEM((size,), F32) for size in sizes]
-        + [pltpu.SemaphoreType.DMA((46,))],
+        + [pltpu.SemaphoreType.DMA((34,))],
         compiler_params=pltpu.CompilerParams(vmem_limit_bytes=62 * 2**20),
         name="results",
     )(*results)

time: 66.5 us -> 65.9 us (level)
  no operation moved by 1% of the time
where the time goes in v4:
time: 65.9 us; the launch traced here: 65.7 us
  Pallas kernels  64.2 us (97%)
  between operations  1.5 us (2%)
    pallas_call x1, Pallas kernels, fused_shards(): pl.pallas_call(functools.partial(fused_kernel, (images_here, captions_her...  60 us
    pallas_call x1, Pallas kernels, fused_shards(): pl.pallas_call(functools.partial(finish_kernel, 1.0 / (images_here * dp_s...  4.19 us

profile of v4, /device:TPU:0, one launch (start us, length us, event | category | flops | bytes accessed | tf_op | source)
XLA Modules:
  0.0 65.7 jit_solution(4022322744823326421)
XLA Ops:
  1.3 60.0 %fused_block.1 = (bf16[800,768]{1,0:T(8,128)(2,1)}, f32[800,768]{1,0:T(8,128)}, f32[96,576]{1,0:T(8,128)}, f32[96,192]{1,0:T(8,128)}, f32[96,768]{1,0:T(8,128)},...) custom-call(bf16[800,768]{1,0:T(8,128)(2,1)} %bitcast.11, ...), custom_call_target="tpu_custom_call" | custom-call | tf_op jit(solution)/shard_map/fused_block/pallas_call | solution.py:1047
  61.3 4.2 %results.1 = (bf16[800,768]{1,0:T(8,128)(2,1)}, f32[800,768]{1,0:T(8,128)}, f32[96,576]{1,0:T(8,128)}, f32[96,192]{1,0:T(8,128)}, f32[96,768]{1,0:T(8,128)}, /*i...) custom-call(bf16[800,768]{1,0:T(8,128)(2,1)} %get-tuple-element.50.r, ...), custom_call_target="tpu_custom_call" | custom-call | tf_op jit(solution)/shard_map/results/pallas_call | solution.py:1064
